TPU v7x, 128 devices: a whole 4x4x4 slice. The times are simulated.
128 devices in a mesh: shard: 32 (over z, x, core), grp: 4 (over y).
Axes of the slice: x: 4, y: 4, z: 4, core: 2. Of those that a mesh axis runs over, the one named last changes fastest.
Arguments:
- query_states: bfloat16 [512, 32, 1024], P(('shard', 'grp')), may hold values from -6 to 6
- norm_gain: float32 [1024], replicated, may hold values from 0.25 to 1.75
- final_gain: float32 [1024], replicated, may hold values from 0.25 to 1.75
- w_gate: bfloat16 [1024, 2624], P(None, 'grp'), may hold values from -0.1875 to 0.1875
- w_up: bfloat16 [1024, 2624], P(None, 'grp'), may hold values from -0.1875 to 0.1875
- w_down_t: bfloat16 [1024, 2624], P(None, 'grp'), may hold values from -0.125 to 0.125
- w_proj: bfloat16 [1024, 128], replicated, may hold values from -0.1875 to 0.1875
- centroids: bfloat16 [128, 262144], P('grp'), may hold values from -0.52734375 to 0.52734375
- bucket_values: float32 [4, 128], P(None, 'grp'), may hold values from -0.26516503 to 0.26516503
- centroid_ids: int32 [4096, 128], P('shard'), may hold values from 0 to 262143
- residual_codes: int32 [4096, 16, 128], P('shard', 'grp'), may hold values from 0 to 65535
- passage_lens: int32 [4096], replicated, may hold values from 16 to 128
- negative_ids: int32 [512, 16], P(('shard', 'grp')), may hold values from 0 to 4095, as said below
Outputs:
- losses: float32 [512], P(('shard', 'grp'))
- grad_gate: float32 [1024, 2624], P('shard', 'grp')
- grad_up: float32 [1024, 2624], P('shard', 'grp')
- grad_down: float32 [1024, 2624], P('shard', 'grp')
- grad_proj: float32 [1024, 128], P(('shard', 'grp'))
Inputs may be any that keep to these rules, and one draw needn't show every extreme that they name: `negative_ids`: passage id p lies in index shard p // 128. The 16 candidates of the 4 queries of one device name at most 4 passages of any one index shard, counted with repeats; one index shard, the same for all devices, is named exactly 4 times by every device.
All inputs are finite; a program needn't handle non-finite values.
Results may differ from a plain program's by a relative error of at most 0.029.
Values may be sent and summed in bfloat16 or wider, within the bound.
A program may use at most 256 MiB of HBM per device.

v0:
```python
import math

import jax
import jax.numpy as jnp
from jax import lax
from jax.sharding import PartitionSpec as P


def layer_norm(rows, gain):
    centre = rows - jnp.mean(rows, axis=-1, keepdims=True)
    spread = jnp.mean(centre * centre, axis=-1, keepdims=True)
    return centre * lax.rsqrt(spread + 1e-05) * gain


def gelu_exact(values):
    return 0.5 * values * (1.0 + jax.scipy.special.erf(values / math.sqrt(2.0)))


def gelu_slope(values):
    cdf = 0.5 * (1.0 + jax.scipy.special.erf(values / math.sqrt(2.0)))
    return cdf + values * jnp.exp(-0.5 * values * values) / math.sqrt(2.0 * math.pi)


def pack_table(table):
    dim_part, count = table.shape
    grouped = jnp.transpose(table.reshape(dim_part, count // 4, 4), (1, 2, 0))
    return grouped.reshape(count // 4, 4 * dim_part)


def rebuild(pass_ids, packed, codes, bucket, cent_ids):
    cids = cent_ids[pass_ids]
    words = codes[pass_ids]
    dim_part = bucket.shape[1]
    flat = cids.reshape(-1)
    fetched = packed[flat // 4].reshape(flat.shape[0], 4, dim_part)
    pick = (flat % 4)[:, None] == lax.broadcasted_iota(jnp.int32, (1, 4), 1)
    base = jnp.sum(
        jnp.where(pick[:, :, None], fetched.astype(jnp.float32), jnp.float32(0.0)), axis=1
    )
    base = jnp.transpose(base.reshape(cids.shape[0], cids.shape[1], dim_part), (0, 2, 1))
    shifts = 2 * jnp.arange(8)
    fields = jnp.bitwise_and(jnp.right_shift(words[:, :, None, :], shifts[None, None, :, None]), 3)
    fields = fields.reshape(words.shape[0], words.shape[1] * 8, words.shape[2])
    resid = jnp.zeros(fields.shape, jnp.float32)
    for level in range(4):
        resid = resid + jnp.where(fields == level, bucket[level][None, :, None], jnp.float32(0.0))
    return (base + resid).astype(jnp.bfloat16)


def rebuild_blocks(order, blocks, table, codes, bucket, cent_ids):
    packed = pack_table(table)
    pieces = lax.map(
        lambda ids: rebuild(ids, packed, codes, bucket, cent_ids), order.reshape(blocks, -1)
    )
    return pieces.reshape(order.shape[0], table.shape[0], cent_ids.shape[1])


def unit_docs(raw):
    values = raw.astype(jnp.float32)
    width = values.shape[-2]
    scale = lax.rsqrt(jnp.mean(values * values, axis=-2, keepdims=True) + 1e-06) / math.sqrt(width)
    return (values * scale).astype(jnp.bfloat16)


def candidate_losses(proj_rows, docs, doc_lens):
    width = proj_rows.shape[-1]
    scale = lax.rsqrt(jnp.mean(proj_rows * proj_rows, axis=-1, keepdims=True) + 1e-06) / math.sqrt(
        width
    )
    queries = (proj_rows * scale).astype(jnp.bfloat16)
    sims = jnp.einsum("kid,kcdj->kicj", queries, docs, preferred_element_type=jnp.float32)
    spots = lax.broadcasted_iota(jnp.int32, (1, 1, 1, docs.shape[-1]), 3)
    valid = spots < doc_lens[:, None, :, None]
    logits = jnp.where(valid, 64.0 * sims, jnp.float32(-1e30))
    top = lax.stop_gradient(jnp.max(logits, axis=-1, keepdims=True))
    soft = (top[..., 0] + jnp.log(jnp.sum(jnp.exp(logits - top), axis=-1))) / 64.0
    scores = 10.0 * jnp.sum(soft, axis=1)
    ctop = lax.stop_gradient(jnp.max(scores, axis=-1, keepdims=True))
    total = ctop[:, 0] + jnp.log(jnp.sum(jnp.exp(scores - ctop), axis=-1))
    return total - scores[:, 0]


def local(
    query_states,
    norm_gain,
    final_gain,
    w_gate,
    w_up,
    w_down_t,
    w_proj,
    centroids,
    bucket_values,
    centroid_ids,
    residual_codes,
    passage_lens,
    negative_ids,
):
    q_dev, q_len, width = query_states.shape
    dim = w_proj.shape[1]
    shards = lax.axis_size("shard")
    groups = lax.axis_size("grp")
    cands = negative_ids.shape[1]
    tok_rows = q_dev * q_len
    rows = query_states.reshape(tok_rows, width).astype(jnp.float32)
    normed = layer_norm(rows, norm_gain).astype(jnp.bfloat16)
    group_rows = lax.all_gather(normed, "grp", axis=0, tiled=True)
    gate = jnp.dot(group_rows, w_gate, preferred_element_type=jnp.float32)
    up = jnp.dot(group_rows, w_up, preferred_element_type=jnp.float32)
    hidden = (gelu_exact(gate) * up).astype(jnp.bfloat16)
    out = rows + lax.psum_scatter(
        lax.dot_general(
            hidden, w_down_t, (((1,), (1,)), ((), ())), preferred_element_type=jnp.float32
        ),
        "grp",
        scatter_dimension=0,
        tiled=True,
    )
    final = layer_norm(out, final_gain).astype(jnp.bfloat16)
    proj = jnp.dot(final, w_proj, preferred_element_type=jnp.float32).reshape(q_dev, q_len, dim)
    local_pass = centroid_ids.shape[0]
    slots_per = 2 * q_dev * cands // shards
    flat_ids = negative_ids.reshape(-1)
    owner = flat_ids // local_pass
    within = flat_ids - owner * local_pass
    hits = (owner[:, None] == lax.broadcasted_iota(jnp.int32, (1, shards), 1)).astype(jnp.int32)
    before = jnp.cumsum(hits, axis=0) - hits
    rank = jnp.sum(before * hits, axis=1)
    slot = owner * slots_per + rank
    wanted = (
        jnp.zeros((shards * slots_per,), jnp.int32)
        .at[slot]
        .set(within)
        .reshape(1, shards, slots_per)
    )
    group_wanted = lax.all_gather(wanted, "grp", axis=0, tiled=True)
    arrived = lax.all_to_all(group_wanted, "shard", split_axis=1, concat_axis=1, tiled=True)
    dim_part = centroids.shape[0]
    tokp = centroid_ids.shape[1]
    order = jnp.transpose(arrived, (1, 2, 0)).reshape(-1)
    raw = rebuild_blocks(order, groups, centroids, residual_codes, bucket_values, centroid_ids)
    raw = raw.reshape(shards, slots_per, groups, dim_part, tokp)
    landed = lax.all_to_all(
        lax.all_to_all(raw, "shard", split_axis=0, concat_axis=0, tiled=True),
        "grp",
        split_axis=2,
        concat_axis=2,
        tiled=True,
    )
    landed = landed.reshape(shards * slots_per, dim, tokp)
    docs = unit_docs(landed[slot]).reshape(q_dev, cands, dim, tokp)
    lens = passage_lens[flat_ids].reshape(q_dev, cands)
    losses, pull = jax.vjp(lambda v: candidate_losses(v, docs, lens), proj)
    (dproj,) = pull(jnp.ones_like(losses))
    dproj_b = dproj.reshape(tok_rows, dim).astype(jnp.bfloat16)
    contract = (((0,), (0,)), ((), ()))
    proj_term = lax.dot_general(final, dproj_b, contract, preferred_element_type=jnp.float32)
    grad_proj = lax.psum_scatter(proj_term, ("shard", "grp"), scatter_dimension=0, tiled=True)
    dfinal = lax.dot_general(
        dproj_b, w_proj, (((1,), (1,)), ((), ())), preferred_element_type=jnp.float32
    )
    _, pull_norm = jax.vjp(lambda v: layer_norm(v, final_gain), out)
    (dout,) = pull_norm(dfinal)
    dout_b = dout.astype(jnp.bfloat16)
    group_grad = lax.all_gather(dout_b, "grp", axis=0, tiled=True)
    dhid = jnp.dot(group_grad, w_down_t, preferred_element_type=jnp.float32)
    dgate = (dhid * up * gelu_slope(gate)).astype(jnp.bfloat16)
    dup = (dhid * gelu_exact(gate)).astype(jnp.bfloat16)
    term_gate = lax.dot_general(group_rows, dgate, contract, preferred_element_type=jnp.float32)
    term_up = lax.dot_general(group_rows, dup, contract, preferred_element_type=jnp.float32)
    term_down = lax.dot_general(group_grad, hidden, contract, preferred_element_type=jnp.float32)
    grad_gate, grad_up, grad_down = (
        lax.psum_scatter(
            term_gate.astype(jnp.bfloat16), "shard", scatter_dimension=0, tiled=True
        ).astype(jnp.float32),
        lax.psum_scatter(
            term_up.astype(jnp.bfloat16), "shard", scatter_dimension=0, tiled=True
        ).astype(jnp.float32),
        lax.psum_scatter(
            term_down.astype(jnp.bfloat16), "shard", scatter_dimension=0, tiled=True
        ).astype(jnp.float32),
    )
    return (losses, grad_gate, grad_up, grad_down, grad_proj)


def solution(mesh):
    placed = (
        P(("shard", "grp"), None, None),
        P(),
        P(),
        P(None, "grp"),
        P(None, "grp"),
        P(None, "grp"),
        P(),
        P("grp", None),
        P(None, "grp"),
        P("shard", None),
        P("shard", "grp", None),
        P(),
        P(("shard", "grp"), None),
    )
    return jax.shard_map(
        local,
        mesh=mesh,
        in_specs=placed,
        out_specs=(
            P(("shard", "grp")),
            P("shard", "grp"),
            P("shard", "grp"),
            P("shard", "grp"),
            P(("shard", "grp"), None),
        ),
        check_vma=False,
    )
```

profile of v0, /device:TPU:0, one launch (start us, length us, event | category | flops | bytes accessed | tf_op | source)
XLA Modules:
  0.0 1060.4 jit_solution(12625910704525563240)
XLA Ops:
  11.2 11.3 %all_gather.10 = s32[4,32,4]{1,2,0:T(4,128)S(1)} all-gather(s32[1,32,4]{1,2,0:T(4,128)S(1)} %copy.47), channel_id=1, replica_groups=mesh['shard'=32,'grp'=4] {'grp'}, dimensions={0}, use_global_device_ids=true | all-gather | bytes 2560 | tf_op jit(solution)/shard_map/all_gather | solution.py:135
  23.2 8.2 all-to-all-start
  35.8 49.1 %copy.50 = bf16[32,262144]{0,1:T(8,128)(2,1)} copy(bf16[32,262144]{1,0:T(8,128)(2,1)} %param.22) | data formatting | bytes 33554432 | tf_op args[7]
  84.9 77.9 %copy.51 = bf16[65536,4,32]{0,2,1:T(8,128)(2,1)} copy(bf16[65536,4,32]{2,1,0:T(4,128)(2,1)} %bitcast.22) | data formatting | bytes 33554432 | tf_op jit(solution)/shard_map/transpose | solution.py:26
  162.8 22.5 %copy.52 = bf16[65536,128]{1,0:T(8,128)(2,1)} copy(bf16[65536,128]{0,1:T(8,128)(2,1)} %bitcast.149) | data formatting | bytes 33554432 | tf_op jit(solution)/shard_map/while | solution.py:52
  185.7 319.1 %while.12 = (s32[]{:T(128)}, bf16[4,128,32,128]{3,2,1,0:T(8,128)(2,1)}, s32[4,128]{1,0:T(4,128)S(1)}, s32[128,128]{1,0:T(8,128)S(1)}, bf16[65536,128]{1,0:T(8,12...) while((s32[]{:T(128)}, bf16[4,128,32,128]{3,2,1,0:T(8,128)(2,1)}, ...), condition=%wide.region_11.12_spmd, body=%wide.region_9.11_spmd.sunk | while | flops 12092810 | bytes 43000484 | solution.py:52
  187.7 62.9 %gather_fusion.2 = bf16[16384,128]{1,0:T(8,128)(2,1)} fusion(bf16[65536,128]{1,0:T(8,128)(2,1)} %get-tuple-element.233, s32[16384]{0:T(1024)S(1)} %broadcast_clamp_fusion.2), kind=kCustom, calls=%fused_computation.1.clone.1 | custom fusion | bytes 8454144 | tf_op jit(solution)/shard_map/while/body/eval_jaxpr/gather | solution.py:35
  250.6 7.0 copy.68
  267.4 62.9 %gather_fusion.2 = bf16[16384,128]{1,0:T(8,128)(2,1)} fusion(bf16[65536,128]{1,0:T(8,128)(2,1)} %get-tuple-element.233, s32[16384]{0:T(1024)S(1)} %broadcast_clamp_fusion.2), kind=kCustom, calls=%fused_computation.1.clone.1 | custom fusion | bytes 8454144 | tf_op jit(solution)/shard_map/while/body/eval_jaxpr/gather | solution.py:35
  330.3 7.0 copy.68
  347.2 62.9 %gather_fusion.2 = bf16[16384,128]{1,0:T(8,128)(2,1)} fusion(bf16[65536,128]{1,0:T(8,128)(2,1)} %get-tuple-element.233, s32[16384]{0:T(1024)S(1)} %broadcast_clamp_fusion.2), kind=kCustom, calls=%fused_computation.1.clone.1 | custom fusion | bytes 8454144 | tf_op jit(solution)/shard_map/while/body/eval_jaxpr/gather | solution.py:35
  410.1 7.0 copy.68
  427.0 62.9 %gather_fusion.2 = bf16[16384,128]{1,0:T(8,128)(2,1)} fusion(bf16[65536,128]{1,0:T(8,128)(2,1)} %get-tuple-element.233, s32[16384]{0:T(1024)S(1)} %broadcast_clamp_fusion.2), kind=kCustom, calls=%fused_computation.1.clone.1 | custom fusion | bytes 8454144 | tf_op jit(solution)/shard_map/while/body/eval_jaxpr/gather | solution.py:35
  489.9 7.0 copy.68
  504.9 7.3 all-to-all-start.1
  520.5 45.1 %all-to-all-done.1 = bf16[32,4,4,32,128]{4,3,2,1,0:T(8,128)(2,1)} async-done(((bf16[32,4,4,32,128]{4,3,2,1,0:T(8,128)(2,1)}), bf16[32,4,4,32,128]{4,3,2,1,0:T(8,128)(2,1)}, u32[]{:S(2)}, u32[]{:S(2)}) %all-to-all-start.1) | async-done | bytes 4194336 | tf_op jit(solution)/shard_map/all_to_all | solution.py:143
  565.6 5.5 copy.54
  582.0 40.5 %all-to-all-done.2 = bf16[32,4,4,32,128]{4,3,1,0,2:T(8,128)(2,1)} async-done(((bf16[32,4,4,32,128]{4,3,1,0,2:T(8,128)(2,1)}), bf16[32,4,4,32,128]{4,3,1,0,2:T(8,128)(2,1)}, u32[]{:S(2)}, u32[]{:S(2)}) %all-to-all-start.2) | async-done | bytes 4194336 | tf_op jit(solution)/shard_map/all_to_all | solution.py:142
  622.4 5.4 copy.55
  638.1 20.8 %all-gather.5.cloned.1.call-done = bf16[512,1024]{1,0:T(8,128)(2,1)} async-done(((bf16[128,1024]{1,0:T(8,128)(2,1)}), bf16[512,1024]{1,0:T(8,128)(2,1)}) %all-gather.5.cloned.1.call-update) | async-done | bytes 1048592 | tf_op jit(solution)/shard_map/all_gather | solution.py:164
  672.9 136.3 %all-reduce.3.cloned.1.call-done = f32[1024,128]{1,0:T(8,128)} async-done(((f32[1024,128]{1,0:T(8,128)}), f32[1024,128]{1,0:T(8,128)}) %all-reduce.3.cloned.1.call-update) | async-done | bytes 524304
  810.5 79.6 %reduce-scatter.7.cloned.1.call-done = bf16[32,656]{1,0:T(8,128)(2,1)} async-done(((bf16[1024,656]{1,0:T(8,128)(2,1)}), bf16[32,656]{1,0:T(8,128)(2,1)}) %reduce-scatter.7.cloned.1.call-update) | async-done | bytes 42000 | tf_op jit(solution)/shard_map/reduce_scatter | solution.py:172
  891.5 79.5 %reduce-scatter.9.cloned.1.call-done = bf16[32,656]{1,0:T(8,128)(2,1)} async-done(((bf16[1024,656]{1,0:T(8,128)(2,1)}), bf16[32,656]{1,0:T(8,128)(2,1)}) %reduce-scatter.9.cloned.1.call-update) | async-done | bytes 42000 | tf_op jit(solution)/shard_map/reduce_scatter | solution.py:175
  972.5 79.6 %reduce-scatter.11.cloned.1.call-done = bf16[32,656]{1,0:T(8,128)(2,1)} async-done(((bf16[1024,656]{1,0:T(8,128)(2,1)}), bf16[32,656]{1,0:T(8,128)(2,1)}) %reduce-scatter.11.cloned.1.call-update) | async-done | bytes 42000 | tf_op jit(solution)/shard_map/reduce_scatter | solution.py:178
  (206 shorter events, 97.4 us)
Async XLA Ops:
  7.2 510.9 %copy-start = (bf16[1024,656]{0,1:T(8,128)(2,1)S(1)}, bf16[1024,656]{0,1:T(8,128)(2,1)}, u32[]{:S(2)}) copy-start(bf16[1024,656]{0,1:T(8,128)(2,1)} %param.20) | copy-start | bytes 4030468
  23.2 162.0 %all-to-all-start = ((s32[4,32,4]{2,0,1:T(4,128)}), s32[4,32,4]{2,0,1:T(4,128)S(1)}, u32[]{:S(2)}, u32[]{:S(2)}) async-start(s32[4,32,4]{2,0,1:T(4,128)} %copy.48), calls=%async_computation.1 | async-start | bytes 131072 | tf_op jit(solution)/shard_map/all_to_all | solution.py:136
  31.4 481.0 %all-gather.3.cloned.1.call-start = ((), (), s32[]{:S(2)}) async-start(), calls=%async_computation.7 | async-start | bytes 1310720 | tf_op jit(solution)/shard_map/all_gather | solution.py:106
  162.8 22.9 %copy-start.1 = (s32[128,128]{1,0:T(8,128)S(1)}, s32[128,128]{1,0:T(8,128)}, u32[]{:S(2)}) copy-start(s32[128,128]{1,0:T(8,128)} %param.24) | copy-start | bytes 196612
  162.8 22.9 %copy-start.6 = (s32[128,4,128]{2,1,0:T(4,128)S(1)}, s32[128,4,128]{2,1,0:T(4,128)}, u32[]{:S(2)}) copy-start(s32[128,4,128]{2,1,0:T(4,128)} %param.25) | copy-start | bytes 786436
  162.8 22.9 %copy-start.19 = (f32[4,32]{1,0:T(4,128)S(1)}, f32[4,32]{1,0:T(4,128)}, u32[]{:S(2)}) copy-start(f32[4,32]{1,0:T(4,128)} %param.23) | copy-start | bytes 1540
  504.9 60.8 %all-to-all-start.1 = ((bf16[32,4,4,32,128]{4,3,2,1,0:T(8,128)(2,1)}), bf16[32,4,4,32,128]{4,3,2,1,0:T(8,128)(2,1)}, u32[]{:S(2)}, u32[]{:S(2)}) async-start(bf16[32,4,4,32,128]{4,3,2,1,0:T(8,128)(2,1)} %bitcast.155), calls=%async_computation.2 | async-start | bytes 8388608 | tf_op jit(solution)/shard_map/all_to_all | solution.py:143
  512.1 65.0 %reduce-scatter.5.cloned.1.call-start = ((), (), s32[]{:S(2)}) async-start(), calls=%async_computation.8 | async-start | bytes 2621440 | tf_op jit(solution)/shard_map/reduce_scatter | solution.py:110
  571.1 5.1 copy-start.23
  571.1 5.1 copy-start.4
  571.1 6.0 copy-start.22
  571.1 6.1 copy-start.2
  571.1 51.3 %all-to-all-start.2 = ((bf16[32,4,4,32,128]{4,3,1,0,2:T(8,128)(2,1)}), bf16[32,4,4,32,128]{4,3,1,0,2:T(8,128)(2,1)}, u32[]{:S(2)}, u32[]{:S(2)}) async-start(bf16[32,4,4,32,128]{4,3,1,0,2:T(8,128)(2,1)} %copy.54), calls=%async_computation.3 | async-start | bytes 8388608 | tf_op jit(solution)/shard_map/all_to_all | solution.py:142
  576.1 3.5 copy-start.20
  576.1 5.4 copy-start.17
  576.1 82.7 %all-gather.5.cloned.1.call-start = ((), (), s32[]{:S(2)}) async-start(), calls=%async_computation.9 | async-start | bytes 1310720 | tf_op jit(solution)/shard_map/all_gather | solution.py:164
  636.9 172.3 %all-reduce.3.cloned.1.call-start = ((), (), s32[]{:S(2)}) async-start(), calls=%async_computation.13 | async-start | bytes 1048576
  638.1 24.2 %copy-start.8 = (f32[512,656]{0,1:T(8,128)S(1)}, f32[512,656]{0,1:T(8,128)}, u32[]{:S(2)}) copy-start(f32[512,656]{0,1:T(8,128)} %copy-done.7) | copy-start | bytes 4030468
  638.1 252.0 %reduce-scatter.7.cloned.1.call-start = ((), (), s32[]{:S(2)}) async-start(), calls=%async_computation.10 | async-start | bytes 1622016 | tf_op jit(solution)/shard_map/reduce_scatter | solution.py:172
  658.9 3.4 copy-start.9
  658.9 3.4 copy-start.13
  664.8 4.1 copy-start.15
  664.8 306.3 %reduce-scatter.9.cloned.1.call-start = ((), (), s32[]{:S(2)}) async-start(), calls=%async_computation.11 | async-start | bytes 1622016 | tf_op jit(solution)/shard_map/reduce_scatter | solution.py:175
  668.8 383.3 %reduce-scatter.11.cloned.1.call-start = ((), (), s32[]{:S(2)}) async-start(), calls=%async_computation.12 | async-start | bytes 1622016 | tf_op jit(solution)/shard_map/reduce_scatter | solution.py:178
  (12 other events, 19.7 us)
Sparse Core Ops, SparseCore 0:
  35.9 24.4 all-gather.2
  520.6 30.0 reduce-scatter.4
  637.0 21.7 all-gather.4
  664.2 144.9 all-reduce.2
  812.6 77.4 reduce-scatter.6
  893.5 77.5 reduce-scatter.8
  974.6 77.5 reduce-scatter.10
where the time goes:
time: 1070 us; the launch traced here: 1060 us
  waiting for transfers between devices  481 us (45%)
  local copies, waits for them, and re-layouts  467 us (44%)
  other arithmetic  41.6 us (4%)
  matrix products  23.3 us (2%)
  starting transfers between devices  20.9 us (2%)
  between operations  14.6 us (1%)
  blocking collectives  11.3 us (1%)
    gather x4, local copies, waits for them, and re-layouts, rebuild(): fetched = packed[flat // 4].reshape(flat.shape[0], 4, dim_part)  252 us
    unnamed x8, waiting for transfers between devices  136 us
    reduce_scatter x1, waiting for transfers between devices, local(): lax.psum_scatter(term_down.astype(jnp.bfloat16), 'shard', scatter_dimensi...  79.6 us
    reduce_scatter x1, waiting for transfers between devices, local(): lax.psum_scatter(term_gate.astype(jnp.bfloat16), 'shard', scatter_dimensi...  79.6 us
    reduce_scatter x1, waiting for transfers between devices, local(): lax.psum_scatter(term_up.astype(jnp.bfloat16), 'shard', scatter_dimension...  79.5 us
    transpose x1, local copies, waits for them, and re-layouts, pack_table(): grouped = jnp.transpose(table.reshape(dim_part, count // 4, 4), (1, 2, 0))  77.9 us
    unnamed x54, local copies, waits for them, and re-layouts  53.6 us
    all_to_all x1, waiting for transfers between devices, local(): lax.all_to_all(raw, 'shard', split_axis=0, concat_axis=0, tiled=True)  45.1 us
  transfers between devices with their start and end apart: 10, of which 7 were waited for; matrix products, arithmetic and copies ran while one was open for 48% of the time, Pallas kernels for 0%

commit v1 on v0

v1 whole, which is shorter than its diff:
```python
import functools
import math

import jax
import jax.numpy as jnp
from jax import lax
from jax.experimental import pallas as pl
from jax.experimental.pallas import tpu as pltpu
from jax.sharding import PartitionSpec as P

MESH = pl.DeviceIdType.MESH


def layer_norm(rows, gain):
    centre = rows - jnp.mean(rows, axis=-1, keepdims=True)
    spread = jnp.mean(centre * centre, axis=-1, keepdims=True)
    return centre * lax.rsqrt(spread + 1e-05) * gain


def gelu_exact(values):
    return 0.5 * values * (1.0 + jax.scipy.special.erf(values / math.sqrt(2.0)))


def gelu_slope(values):
    cdf = 0.5 * (1.0 + jax.scipy.special.erf(values / math.sqrt(2.0)))
    return cdf + values * jnp.exp(-0.5 * values * values) / math.sqrt(2.0 * math.pi)


def rebuild_kernel(blk_ref, lane_ref, codes_ref, bucket_ref, tab_hbm, out_ref, tab, sem):
    parts = sem.shape[0]
    span = tab.shape[1] // parts
    copies = [
        pltpu.make_async_copy(
            tab_hbm.at[:, pl.ds(i * span, span)], tab.at[:, pl.ds(i * span, span)], sem.at[i]
        )
        for i in range(parts)
    ]
    for copy in copies:
        copy.start()
    for copy in copies:
        copy.wait()
    passages, dims, toks = out_ref.shape
    lane = lax.broadcasted_iota(jnp.int32, (dims, toks), 1)
    shift = 2 * lax.broadcasted_iota(jnp.int32, (8, toks), 0)

    def passage(p, carry):
        spot = jnp.broadcast_to(lane_ref[pl.ds(p, 1), :], (dims, toks))
        base = jnp.zeros((dims, toks), jnp.float32)
        for j in range(toks):
            start = pl.multiple_of(blk_ref[p, j] * 128, 128)
            block = tab[:, pl.ds(start, 128)].astype(jnp.float32)
            base = jnp.where(lane == j, jnp.take_along_axis(block, spot, axis=1), base)
        words = codes_ref[p]
        fields = jnp.concatenate(
            [
                jnp.bitwise_and(
                    jnp.right_shift(jnp.broadcast_to(words[w : w + 1], (8, toks)), shift), 3
                )
                for w in range(dims // 8)
            ],
            axis=0,
        )
        resid = jnp.where(
            fields < 2,
            jnp.where(fields == 0, bucket_ref[0], bucket_ref[1]),
            jnp.where(fields == 2, bucket_ref[2], bucket_ref[3]),
        )
        out_ref[p] = (base + resid).astype(jnp.bfloat16)
        return carry

    lax.fori_loop(0, passages, passage, 0)


def rebuild(cent_ids, codes, bucket, table):
    passages, toks = cent_ids.shape
    dims, count = table.shape
    spread = jnp.broadcast_to(bucket[:, :, None], (4, dims, toks))
    return pl.pallas_call(
        rebuild_kernel,
        out_shape=jax.ShapeDtypeStruct((passages, dims, toks), jnp.bfloat16),
        in_specs=[
            pl.BlockSpec(memory_space=pltpu.SMEM),
            pl.BlockSpec(memory_space=pltpu.VMEM),
            pl.BlockSpec(memory_space=pltpu.VMEM),
            pl.BlockSpec(memory_space=pltpu.VMEM),
            pl.BlockSpec(memory_space=pl.ANY),
        ],
        out_specs=pl.BlockSpec(memory_space=pltpu.VMEM),
        scratch_shapes=[pltpu.VMEM((dims, count), jnp.bfloat16), pltpu.SemaphoreType.DMA((8,))],
        compiler_params=pltpu.CompilerParams(vmem_limit_bytes=36 << 20),
        cost_estimate=pl.CostEstimate(flops=0, bytes_accessed=150_000_000, transcendentals=0),
    )(cent_ids >> 7, cent_ids & 127, codes, spread, table)


def pair_kernel(pass_ref, query_ref, lens_ref, docs_ref, q_ref, pull_ref, score_ref):
    sources, caps, q_len, dim = pull_ref.shape
    toks = docs_ref.shape[3]
    spots = lax.broadcasted_iota(jnp.int32, (q_len, toks), 1)

    def source(d, carry):
        for k in range(caps):
            p = pass_ref[d, k]
            raw = jnp.concatenate([docs_ref[g, p] for g in range(docs_ref.shape[0])], axis=0)
            values = raw.astype(jnp.float32)
            scale = lax.rsqrt(jnp.mean(values * values, axis=0, keepdims=True) + 1e-06) / math.sqrt(dim)
            sims = jnp.dot(q_ref[d, query_ref[d, k]], raw, preferred_element_type=jnp.float32)
            raised = jnp.where(spots < lens_ref[p], jnp.exp(64.0 * (sims * scale)), 0.0)
            total = jnp.sum(raised, axis=1, keepdims=True)
            soft = jnp.sum(jnp.log(total), axis=0, keepdims=True) / 64.0
            weights = (raised * (scale / total)).astype(jnp.bfloat16)
            pull_ref[d, k] = lax.dot_general(
                weights, raw, (((1,), (1,)), ((), ())), preferred_element_type=jnp.float32
            ).astype(jnp.bfloat16)
            score_ref[d, pl.ds(k, 1), :] = jnp.broadcast_to(soft, (1, dim))
        return carry

    lax.fori_loop(0, sources, source, 0)


def pairs(slot_pass, slot_query, lens, docs, queries):
    sources, caps = slot_pass.shape
    q_len, dim = queries.shape[2:]
    return pl.pallas_call(
        pair_kernel,
        out_shape=(
            jax.ShapeDtypeStruct((sources, caps, q_len, dim), jnp.bfloat16),
            jax.ShapeDtypeStruct((sources, caps, dim), jnp.float32),
        ),
        in_specs=[pl.BlockSpec(memory_space=pltpu.SMEM)] * 3
        + [pl.BlockSpec(memory_space=pltpu.VMEM)] * 2,
        out_specs=(pl.BlockSpec(memory_space=pltpu.VMEM),) * 2,
        compiler_params=pltpu.CompilerParams(vmem_limit_bytes=24 << 20),
        cost_estimate=pl.CostEstimate(flops=0, bytes_accessed=40_000_000, transcendentals=0),
    )(slot_pass, slot_query, lens, docs, queries)


def coords(shape):
    me = lax.axis_index("shard")
    return me // (2 * shape), (me // 2) % shape, me % 2, lax.axis_index("grp")


def scatter_kernel(
    side, groups, gate_ref, up_ref, down_ref, proj_ref, gate_out, up_out, down_out, proj_out,
    twin, twin_proj, held, held_proj, land, land_proj, rows_sum, land_grp,
    twin_send, twin_recv, chip_send, chip_recv, grp_send, grp_recv,
):
    z, x, core, grp = coords(side)
    chips = side * side
    chip = z * side + x
    sibling = (chip * 2 + 1 - core, grp)

    def peer(step):
        other = ((z + step // side) % side) * side + (x + step % side) % side
        return other, (other * 2 + core, grp)

    barrier = pltpu.get_barrier_semaphore()
    pl.semaphore_signal(barrier, inc=1, device_id=sibling, device_id_type=MESH)
    for step in range(1, chips):
        pl.semaphore_signal(barrier, inc=1, device_id=peer(step)[1], device_id_type=MESH)
    for step in range(1, groups):
        pl.semaphore_signal(
            barrier, inc=1, device_id=(chip * 2 + core, (grp + step) % groups), device_id_type=MESH
        )
    pl.semaphore_wait(barrier, chips + groups - 1)

    terms = (gate_ref, up_ref, down_ref)

    def swap(src, dst, i):
        return pltpu.make_async_remote_copy(
            src_ref=src, dst_ref=dst, send_sem=twin_send.at[i], recv_sem=twin_recv.at[i],
            device_id=sibling, device_id_type=MESH,
        )

    first = [swap(proj_ref.at[:, 1 - core], twin_proj, 3)]
    first += [swap(terms[i].at[:, 1 - core], twin.at[:, i], i) for i in range(3)]
    for copy in first:
        copy.start()
    first[0].wait_recv()

    def add_proj(c, carry):
        held_proj[c] = proj_ref[c, core] + twin_proj[c]
        return carry

    lax.fori_loop(0, chips, add_proj, 0)
    for i in range(3):
        first[1 + i].wait_recv()

        def add(c, carry):
            held[c, i] = (
                terms[i][c, core].astype(jnp.float32) + twin[c, i].astype(jnp.float32)
            ).astype(jnp.bfloat16)
            return carry

        lax.fori_loop(0, chips, add, 0)

    def send(step, src, dst, kind):
        other, device = peer(step)
        return pltpu.make_async_remote_copy(
            src_ref=src.at[other], dst_ref=dst.at[step - 1],
            send_sem=chip_send.at[kind, step - 1], recv_sem=chip_recv.at[kind, step - 1],
            device_id=device, device_id_type=MESH,
        )

    small = [send(step, held_proj, land_proj, 0) for step in range(1, chips)]
    large = [send(step, held, land, 1) for step in range(1, chips)]
    for copy in small:
        copy.start()
    for copy in large:
        copy.start()
    for copy in small:
        copy.wait_recv()
    total = held_proj[chip]
    for step in range(1, chips):
        total = total + land_proj[step - 1]
    rows_sum[...] = total.reshape(rows_sum.shape)
    last = []
    for step in range(1, groups):
        other = (grp + step) % groups
        last.append(
            pltpu.make_async_remote_copy(
                src_ref=rows_sum.at[other], dst_ref=land_grp.at[step - 1],
                send_sem=grp_send.at[step - 1], recv_sem=grp_recv.at[step - 1],
                device_id=(chip * 2 + core, other), device_id_type=MESH,
            )
        )
        last[-1].start()
    for copy in last:
        copy.wait_recv()
    mine = rows_sum[grp]
    for step in range(1, groups):
        mine = mine + land_grp[step - 1]
    proj_out[...] = mine
    for copy in large:
        copy.wait_recv()
    for i, out in enumerate((gate_out, up_out, down_out)):
        total = held[chip, i].astype(jnp.float32)
        for step in range(1, chips):
            total = total + land[step - 1, i].astype(jnp.float32)
        out[...] = total
    for copy in first + small + large + last:
        copy.wait_send()


def scatter_sums(term_gate, term_up, term_down, proj_term, side):
    groups = lax.axis_size("grp")
    width, part = term_gate.shape
    dim = proj_term.shape[1]
    chips = side * side
    rows = width // (2 * chips)
    terms = [t.reshape(chips, 2, rows, part) for t in (term_gate, term_up, term_down)]
    wide = (chips, 3, rows, part)
    return pl.pallas_call(
        functools.partial(scatter_kernel, side, groups),
        out_shape=(jax.ShapeDtypeStruct((rows, part), jnp.float32),) * 3
        + (jax.ShapeDtypeStruct((rows // groups, dim), jnp.float32),),
        in_specs=[pl.BlockSpec(memory_space=pltpu.VMEM)] * 4,
        out_specs=(pl.BlockSpec(memory_space=pltpu.VMEM),) * 4,
        scratch_shapes=[
            pltpu.VMEM(wide, jnp.bfloat16),
            pltpu.VMEM((chips, rows, dim), jnp.float32),
            pltpu.VMEM(wide, jnp.bfloat16),
            pltpu.VMEM((chips, rows, dim), jnp.float32),
            pltpu.VMEM((chips - 1, 3, rows, part), jnp.bfloat16),
            pltpu.VMEM((chips - 1, rows, dim), jnp.float32),
            pltpu.VMEM((groups, rows // groups, dim), jnp.float32),
            pltpu.VMEM((groups - 1, rows // groups, dim), jnp.float32),
            pltpu.SemaphoreType.DMA((4,)),
            pltpu.SemaphoreType.DMA((4,)),
            pltpu.SemaphoreType.DMA((2, chips - 1)),
            pltpu.SemaphoreType.DMA((2, chips - 1)),
            pltpu.SemaphoreType.DMA((groups - 1,)),
            pltpu.SemaphoreType.DMA((groups - 1,)),
        ],
        compiler_params=pltpu.CompilerParams(
            collective_id=0, has_side_effects=True, vmem_limit_bytes=32 << 20
        ),
        cost_estimate=pl.CostEstimate(flops=0, bytes_accessed=60_000_000, transcendentals=0),
    )(*terms, proj_term.reshape(chips, 2, rows, dim))


def ranks(hits):
    count = hits.shape[1]
    before = lax.broadcasted_iota(jnp.int32, (count, count), 0) < lax.broadcasted_iota(
        jnp.int32, (count, count), 1
    )
    return jnp.dot(
        hits.astype(jnp.bfloat16), before.astype(jnp.bfloat16), preferred_element_type=jnp.float32
    ).astype(jnp.int32)


def slots(hits, caps):
    nth = lax.broadcasted_iota(jnp.int32, (1, caps, 1), 1)
    return hits[:, None, :] & (ranks(hits)[:, None, :] == nth)


def local(
    query_states,
    norm_gain,
    final_gain,
    w_gate,
    w_up,
    w_down_t,
    w_proj,
    centroids,
    bucket_values,
    centroid_ids,
    residual_codes,
    passage_lens,
    negative_ids,
):
    q_dev, q_len, width = query_states.shape
    dim = w_proj.shape[1]
    shards = lax.axis_size("shard")
    groups = lax.axis_size("grp")
    side = math.isqrt(shards // 2)
    cands = negative_ids.shape[1]
    tok_rows = q_dev * q_len
    local_pass = centroid_ids.shape[0]
    caps = 2 * q_dev * cands // shards
    me = lax.axis_index("shard")

    flat_ids = negative_ids.reshape(1, -1)
    column_ids = lax.all_gather(flat_ids, "shard", axis=0, tiled=True)
    rows = query_states.reshape(tok_rows, width).astype(jnp.float32)
    normed = layer_norm(rows, norm_gain).astype(jnp.bfloat16)
    group_rows = lax.all_gather(normed, "grp", axis=0, tiled=True)

    raw = rebuild(centroid_ids, residual_codes, bucket_values, centroids)
    docs = lax.all_gather(raw, "grp", axis=0)

    gate = jnp.dot(group_rows, w_gate, preferred_element_type=jnp.float32)
    up = jnp.dot(group_rows, w_up, preferred_element_type=jnp.float32)
    hidden = (gelu_exact(gate) * up).astype(jnp.bfloat16)
    out = rows + lax.psum_scatter(
        lax.dot_general(
            hidden, w_down_t, (((1,), (1,)), ((), ())), preferred_element_type=jnp.float32
        ),
        "grp",
        scatter_dimension=0,
        tiled=True,
    )
    final = layer_norm(out, final_gain).astype(jnp.bfloat16)
    proj = jnp.dot(final, w_proj, preferred_element_type=jnp.float32)
    length = lax.rsqrt(jnp.mean(proj * proj, axis=-1, keepdims=True) + 1e-06)
    scale = length / math.sqrt(dim)
    queries = (proj * scale).astype(jnp.bfloat16).reshape(1, q_dev, q_len, dim)
    column_queries = lax.all_gather(queries, "shard", axis=0, tiled=True)

    asked = slots(column_ids // local_pass == me, caps)
    places = lax.broadcasted_iota(jnp.int32, (1, 1, q_dev * cands), 2)
    slot_pass = jnp.sum(jnp.where(asked, (column_ids % local_pass)[:, None, :], 0), axis=2)
    slot_query = jnp.sum(jnp.where(asked, places // cands, 0), axis=2)
    lens = lax.dynamic_slice(passage_lens, (me * local_pass,), (local_pass,))
    pull, score = pairs(slot_pass, slot_query, lens, docs, column_queries)
    pull = lax.all_to_all(pull, "shard", split_axis=0, concat_axis=0, tiled=True)
    score = lax.all_to_all(score[:, :, :1], "shard", split_axis=0, concat_axis=0, tiled=True)

    owner = lax.broadcasted_iota(jnp.int32, (shards, 1), 0)
    sent = slots(flat_ids // local_pass == owner, caps)
    filled = jnp.any(sent, axis=2).reshape(1, -1)
    place = jnp.sum(jnp.where(sent, places, 0), axis=2).reshape(1, -1)
    query = lax.broadcasted_iota(jnp.int32, (q_dev, 1), 0)
    mine = filled & (place // cands == query)
    first = mine & (place % cands == 0)
    scores = 10.0 * score.reshape(1, -1)
    top = jnp.max(jnp.where(mine, scores, -jnp.inf), axis=1, keepdims=True)
    raised = jnp.where(mine, jnp.exp(scores - top), 0.0)
    total = jnp.sum(raised, axis=1, keepdims=True)
    losses = (
        top + jnp.log(total) - jnp.sum(jnp.where(first, scores, 0.0), axis=1, keepdims=True)
    ).reshape(q_dev)
    weights = 10.0 * (raised / total - first.astype(jnp.float32))
    high = weights.astype(jnp.bfloat16)
    low = (weights - high.astype(jnp.float32)).astype(jnp.bfloat16)
    both = jnp.dot(
        jnp.concatenate([high, low], axis=0),
        pull.reshape(shards * caps, q_len * dim),
        preferred_element_type=jnp.float32,
    )
    dqueries = (both[:q_dev] + both[q_dev:]).reshape(tok_rows, dim)
    dqueries = dqueries.astype(jnp.bfloat16).astype(jnp.float32)
    along = jnp.mean(dqueries * proj, axis=-1, keepdims=True)
    dproj_b = (scale * (dqueries - proj * (length * length * along))).astype(jnp.bfloat16)

    contract = (((0,), (0,)), ((), ()))
    proj_term = lax.dot_general(final, dproj_b, contract, preferred_element_type=jnp.float32)
    dfinal = lax.dot_general(
        dproj_b, w_proj, (((1,), (1,)), ((), ())), preferred_element_type=jnp.float32
    )
    _, pull_norm = jax.vjp(lambda v: layer_norm(v, final_gain), out)
    (dout,) = pull_norm(dfinal)
    dout_b = dout.astype(jnp.bfloat16)
    group_grad = lax.all_gather(dout_b, "grp", axis=0, tiled=True)
    dhid = jnp.dot(group_grad, w_down_t, preferred_element_type=jnp.float32)
    dgate = (dhid * up * gelu_slope(gate)).astype(jnp.bfloat16)
    dup = (dhid * gelu_exact(gate)).astype(jnp.bfloat16)
    term_gate = lax.dot_general(group_rows, dgate, contract, preferred_element_type=jnp.float32)
    term_up = lax.dot_general(group_rows, dup, contract, preferred_element_type=jnp.float32)
    term_down = lax.dot_general(group_grad, hidden, contract, preferred_element_type=jnp.float32)
    grad_gate, grad_up, grad_down, grad_proj = scatter_sums(
        term_gate.astype(jnp.bfloat16),
        term_up.astype(jnp.bfloat16),
        term_down.astype(jnp.bfloat16),
        proj_term,
        side,
    )
    return (losses, grad_gate, grad_up, grad_down, grad_proj)


def solution(mesh):
    placed = (
        P(("shard", "grp"), None, None),
        P(),
        P(),
        P(None, "grp"),
        P(None, "grp"),
        P(None, "grp"),
        P(),
        P("grp", None),
        P(None, "grp"),
        P("shard", None),
        P("shard", "grp", None),
        P(),
        P(("shard", "grp"), None),
    )
    return jax.shard_map(
        local,
        mesh=mesh,
        in_specs=placed,
        out_specs=(
            P(("shard", "grp")),
            P("shard", "grp"),
            P("shard", "grp"),
            P("shard", "grp"),
            P(("shard", "grp"), None),
        ),
        check_vma=False,
    )
```

time: 1070 us -> 361 us (0.34)
  local copies, waits for them, and re-layouts: 467 us -> 27.4 us
  waiting for transfers between devices: 481 us -> 135 us
  Pallas kernels: 0 us -> 115 us
  other arithmetic: 41.6 us -> 14.1 us
  starting transfers between devices: 20.9 us -> 9.51 us
    gather x18 -> x0, local copies, waits for them, and re-layouts: 261 us -> none  [the longest x4 252 us: rebuild(): fetched = packed[flat // 4].reshape(flat.shape[0], 4, dim_part)]
    reduce_scatter x3 -> x0, waiting for transfers between devices: 239 us -> none  [the longest x1 79.6 us: local(): lax.psum_scatter(term_down.astype(jnp.bfloat16), 'shard', scatter_dimensi...]
    unnamed x8 -> x5, waiting for transfers between devices: 136 us -> 0.08 us
    pallas_call x0 -> x3, Pallas kernels: none -> 115 us  [the longest x1 49.3 us: rebuild(): pl.pallas_call(rebuild_kernel, out_shape=jax.ShapeDtypeStruct((passages,...]
    transpose x2 -> x0, local copies, waits for them, and re-layouts: 78.3 us -> none  [the longest x1 77.9 us: pack_table(): grouped = jnp.transpose(table.reshape(dim_part, count // 4, 4), (1, 2, 0))]
    all_gather x0 -> x2, waiting for transfers between devices: none -> 67.6 us  [the longest x1 46.2 us: local(): column_queries = lax.all_gather(queries, 'shard', axis=0, tiled=True)]
    all_to_all x3 -> x2, waiting for transfers between devices: 85.5 us -> 19.7 us  [the longest x1 13.5 us: local(): lax.all_to_all(pull, 'shard', split_axis=0, concat_axis=0, tiled=True)]
    unnamed x54 -> x61, local copies, waits for them, and re-layouts: 53.6 us -> 17.4 us
  transfers between devices with their start and end apart: 10 -> 7, of which waited for: 7 -> 6; matrix products, arithmetic and copies ran while one was open for 48% -> 3% of each run, Pallas kernels for 0% -> 14%
where the time goes in v1:
time: 361 us; the launch traced here: 357 us
  waiting for transfers between devices  135 us (37%)
  Pallas kernels  115 us (32%)
  local copies, waits for them, and re-layouts  27.4 us (8%)
  blocking collectives  21.6 us (6%)
  matrix products  20.6 us (6%)
  between operations  14.2 us (4%)
  other arithmetic  14.1 us (4%)
  starting transfers between devices  9.51 us (3%)
    pallas_call x1, Pallas kernels, rebuild(): pl.pallas_call(rebuild_kernel, out_shape=jax.ShapeDtypeStruct((passages,...  49.3 us
    all_gather x1, waiting for transfers between devices, local(): column_queries = lax.all_gather(queries, 'shard', axis=0, tiled=True)  46.2 us
    pallas_call x1, Pallas kernels, scatter_sums(): pl.pallas_call(functools.partial(scatter_kernel, side, groups), out_shape...  45.1 us
    all_gather x1, waiting for transfers between devices, local(): group_rows = lax.all_gather(normed, 'grp', axis=0, tiled=True)  26.5 us
    all_gather x1, blocking collectives, local(): column_ids = lax.all_gather(flat_ids, 'shard', axis=0, tiled=True)  21.6 us
    all_gather x1, waiting for transfers between devices, local(): docs = lax.all_gather(raw, 'grp', axis=0)  21.5 us
    all_gather x1, waiting for transfers between devices, local(): group_grad = lax.all_gather(dout_b, 'grp', axis=0, tiled=True)  20.9 us
    pallas_call x1, Pallas kernels, pairs(): pl.pallas_call(pair_kernel, out_shape=(jax.ShapeDtypeStruct((sources, cap...  20.5 us
  transfers between devices with their start and end apart: 7, of which 6 were waited for; matrix products, arithmetic and copies ran while one was open for 3% of the time, Pallas kernels for 14%

profile of v1, /device:TPU:0, one launch (start us, length us, event | category | flops | bytes accessed | tf_op | source)
XLA Modules:
  0.0 357.2 jit_solution(11637212863450398744)
XLA Ops:
  9.7 1.9 fusion.17
  11.7 26.5 %all-gather.7.cloned.1.call-done = bf16[512,1024]{1,0:T(8,128)(2,1)} async-done(((bf16[128,1024]{1,0:T(8,128)(2,1)}), bf16[512,1024]{1,0:T(8,128)(2,1)}) %all-gather.7.cloned.1.call-update) | async-done | bytes 1048592 | tf_op jit(solution)/shard_map/all_gather | solution.py:326
  38.3 2.6 fusion.42
  40.9 2.0 multiply_convert_fusion.1
  43.8 2.3 fusion.43
  47.2 5.8 %copy-done.1 = bf16[32,262144]{1,0:T(8,128)(2,1)S(1)} copy-done((bf16[32,262144]{1,0:T(8,128)(2,1)S(1)}, bf16[32,262144]{1,0:T(8,128)(2,1)}, u32[]{:S(2)}) %copy-start.1) | copy-done | bytes 16777240
  52.9 49.3 %shard_map.164 = bf16[128,32,128]{2,1,0:T(8,128)(2,1)} custom-call(s32[128,128]{1,0:T(8,128)S(1)} %get-tuple-element.28.blk_ref, s32[128,128]{1,0:T(8,128)S(1)} %get-tuple-element.27.lane_ref, s32[128,4,128]{2,1,0:T(4,128)S(1)} %copy-done.6, f32[4,32,128]{2,1,0:T(8,128)S(1)} %broadcast_in_dim.83.bucket_ref, bf16[32,262144]{1,0:T(8,128)(2,1)S(1)} %copy-done.1), custom_call_target="tpu_custom_call" | custom-call | bytes 150000000 | tf_op jit(solution)/shard_map/pallas_call | solution.py:78
  106.4 21.6 %all-gather.1 = s32[32,1,64]{2,1,0:T(1,128)S(1)} all-gather(s32[1,1,64]{2,1,0:T(1,128)S(1)} %reshape.361), channel_id=1, replica_groups=mesh['shard'=32,'grp'=4] {'shard'}, dimensions={0}, use_global_device_ids=true | all-gather | bytes 8448 | tf_op jit(solution)/shard_map/all_gather | solution.py:323
  129.6 21.5 %all-gather.13.cloned.1.call-done = bf16[512,32,128]{2,1,0:T(8,128)(2,1)} async-done(((bf16[128,32,128]{2,1,0:T(8,128)(2,1)}), bf16[512,32,128]{2,1,0:T(8,128)(2,1)}) %all-gather.13.cloned.1.call-update) | async-done | bytes 4194320 | tf_op jit(solution)/shard_map/all_gather | solution.py:329
  151.0 46.2 %all-gather.9.cloned.1.call-done.q_ref = bf16[32,4,32,128]{3,2,1,0:T(8,128)(2,1)} async-done(((bf16[1,4,32,128]{3,2,1,0:T(8,128)(2,1)}), bf16[32,4,32,128]{3,2,1,0:T(8,128)(2,1)}) %all-gather.9.cloned.1.call-update) | async-done | bytes 1048592 | tf_op jit(solution)/shard_map/all_gather | solution.py:347
  197.2 2.2 copy-done.4
  200.6 20.5 %shard_map.165 = (bf16[32,4,32,128]{3,2,1,0:T(8,128)(2,1)}, f32[32,4,128]{2,1,0:T(4,128)S(1)}) custom-call(s32[32,4]{1,0:T(8,128)S(1)} %copy.30.pass_ref, s32[32,4]{1,0:T(8,128)S(1)} %copy.31.query_ref, s32[128]{0:T(128)S(1)} %dynamic_slice.3.lens_ref, bf16[4,128,32,128]{3,2,1,0:T(8,128)(2,1)S(1)} %bitcast.55, bf16[32,4,32,128]{3,2,1,0:T(8,128)(2,1)S(1)} %copy-done.5), custom_call_target="tpu_custom_call" | custom-call | bytes 40000000 | tf_op jit(solution)/shard_map/pallas_call | solution.py:123
  222.0 5.2 %all-to-all-start = ((f32[32,4,1]{1,2,0:T(1,128)}), f32[32,4,1]{1,2,0:T(1,128)S(1)}, u32[]{:S(2)}, u32[]{:S(2)}) async-start(f32[32,4,1]{1,2,0:T(1,128)} %copy.32), calls=%async_computation.1 | async-start | bytes 32768 | tf_op jit(solution)/shard_map/all_to_all | solution.py:356
  228.3 6.2 %all-to-all-done = f32[32,4,1]{1,2,0:T(1,128)S(1)} async-done(((f32[32,4,1]{1,2,0:T(1,128)}), f32[32,4,1]{1,2,0:T(1,128)S(1)}, u32[]{:S(2)}, u32[]{:S(2)}) %all-to-all-start) | async-done | bytes 544 | tf_op jit(solution)/shard_map/all_to_all | solution.py:356
  234.5 3.9 %all-to-all-start.1 = ((bf16[32,4,32,128]{3,2,1,0:T(8,128)(2,1)}), bf16[32,4,32,128]{3,2,1,0:T(8,128)(2,1)S(1)}, u32[]{:S(2)}, u32[]{:S(2)}) async-start(bf16[32,4,32,128]{3,2,1,0:T(8,128)(2,1)} %get-tuple-element.12), calls=%async_computation.2 | async-start | bytes 2097152 | tf_op jit(solution)/shard_map/all_to_all | solution.py:355
  242.3 13.5 %all-to-all-done.1 = bf16[32,4,32,128]{3,2,1,0:T(8,128)(2,1)S(1)} async-done(((bf16[32,4,32,128]{3,2,1,0:T(8,128)(2,1)}), bf16[32,4,32,128]{3,2,1,0:T(8,128)(2,1)S(1)}, u32[]{:S(2)}, u32[]{:S(2)}) %all-to-all-start.1) | async-done | bytes 1048608 | tf_op jit(solution)/shard_map/all_to_all | solution.py:355
  259.4 20.9 %all-gather.11.cloned.1.call-done = bf16[512,1024]{1,0:T(8,128)(2,1)} async-done(((bf16[128,1024]{1,0:T(8,128)(2,1)}), bf16[512,1024]{1,0:T(8,128)(2,1)}) %all-gather.11.cloned.1.call-update) | async-done | bytes 1048592 | tf_op jit(solution)/shard_map/all_gather | solution.py:393
  280.3 3.2 convolution_convert_fusion
  285.2 2.3 fusion.44
  288.5 2.0 convolution_convert_fusion.1
  290.5 2.6 copy.34
  293.1 4.7 %convolution_convert_fusion.2 = bf16[1024,656]{0,1:T(8,128)(2,1)} fusion(bf16[512,1024]{1,0:T(8,128)(2,1)} %all-gather.7.cloned.1.call-done, f32[512,656]{0,1:T(8,128)} %copy-done.8, f32[512,656]{0,1:T(8,128)} %copy-done.13, f32[512,656]{0,1:T(8,128)} %get-tuple-element.30), kind=kOutput, calls=%fused_computation.3 | convolution fusion | flops 692232192 | bytes 6422528 | tf_op jit(solution)/shard_map/dot_general | solution.py:397
  297.7 2.5 copy.33
  303.1 45.1 %shard_map.166 = (f32[32,656]{1,0:T(8,128)S(1)}, f32[32,656]{1,0:T(8,128)S(1)}, f32[32,656]{1,0:T(8,128)S(1)}, f32[8,128]{1,0:T(8,128)S(1)}) custom-call(bf16[16,2,32,656]{3,2,1,0:T(8,128)(2,1)S(1)} %bitcast.54, bf16[16,2,32,656]{3,2,1,0:T(8,128)(2,1)S(1)} %bitcast.53, bf16[16,2,32,656]{3,2,1,0:T(8,128)(2,1)S(1)} %bitcast.52, f32[16,2,32,128]{3,2,1,0:T(8,128)S(1)} %bitcast.56), custom_call_target="tpu_custom_call" | custom-call | bytes 60000000 | tf_op jit(solution)/shard_map/pallas_call | solution.py:252
  (126 shorter events, 28.6 us)
Async XLA Ops:
  7.2 36.6 %copy-start = (bf16[1024,656]{0,1:T(8,128)(2,1)S(1)}, bf16[1024,656]{0,1:T(8,128)(2,1)}, u32[]{:S(2)}) copy-start(bf16[1024,656]{0,1:T(8,128)(2,1)} %param.18) | copy-start | bytes 4030468
  7.2 31.1 %all-gather.7.cloned.1.call-start = ((), (), s32[]{:S(2)}) async-start(), calls=%async_computation.3 | async-start | bytes 1310720 | tf_op jit(solution)/shard_map/all_gather | solution.py:326
  11.7 29.2 %copy-start.18 = (bf16[1024,656]{0,1:T(8,128)(2,1)S(1)}, bf16[1024,656]{0,1:T(8,128)(2,1)}, u32[]{:S(2)}) copy-start(bf16[1024,656]{0,1:T(8,128)(2,1)} %param.17) | copy-start | bytes 4030468
  11.7 90.7 %reduce-scatter.2.cloned.1.call-start = ((), (), s32[]{:S(2)}) async-start(), calls=%async_computation.4 | async-start | bytes 2621440 | tf_op jit(solution)/shard_map/reduce_scatter | solution.py:334
  38.3 2.7 copy-start.11
  40.9 2.1 copy-start.8
  46.2 104.9 %all-gather.13.cloned.1.call-start = ((), (), s32[]{:S(2)}) async-start(), calls=%async_computation.7 | async-start | bytes 5242880 | tf_op jit(solution)/shard_map/all_gather | solution.py:329
  47.2 5.8 %copy-start.1 = (bf16[32,262144]{1,0:T(8,128)(2,1)S(1)}, bf16[32,262144]{1,0:T(8,128)(2,1)}, u32[]{:S(2)}) copy-start(bf16[32,262144]{1,0:T(8,128)(2,1)} %tab_hbm.1) | copy-start | bytes 50331652
  52.9 49.5 %copy-start.7 = (bf16[4,32,1024]{2,1,0:T(8,128)(2,1)S(1)}, bf16[4,32,1024]{2,1,0:T(8,128)(2,1)}, u32[]{:S(2)}) copy-start(bf16[4,32,1024]{2,1,0:T(8,128)(2,1)} %param.13) | copy-start | bytes 786436
  102.3 2.7 copy-start.22
  102.3 2.8 copy-start.19
  102.3 94.9 %all-gather.9.cloned.1.call-start = ((), (), s32[]{:S(2)}) async-start(), calls=%async_computation.5 | async-start | bytes 1081344 | tf_op jit(solution)/shard_map/all_gather | solution.py:347
  102.4 2.5 copy-start.10
  103.6 2.5 copy-start.23
  105.1 23.2 %copy-start.14 = (bf16[128,1024]{1,0:T(8,128)(2,1)}, bf16[128,1024]{1,0:T(8,128)(2,1)S(1)}, u32[]{:S(2)}) copy-start(bf16[128,1024]{1,0:T(8,128)(2,1)S(1)} %multiply_convert_fusion.3) | copy-start | bytes 786436
  197.2 2.2 copy-start.4
  222.0 12.5 %all-to-all-start = ((f32[32,4,1]{1,2,0:T(1,128)}), f32[32,4,1]{1,2,0:T(1,128)S(1)}, u32[]{:S(2)}, u32[]{:S(2)}) async-start(f32[32,4,1]{1,2,0:T(1,128)} %copy.32), calls=%async_computation.1 | async-start | bytes 32768 | tf_op jit(solution)/shard_map/all_to_all | solution.py:356
  234.5 21.3 %all-to-all-start.1 = ((bf16[32,4,32,128]{3,2,1,0:T(8,128)(2,1)}), bf16[32,4,32,128]{3,2,1,0:T(8,128)(2,1)S(1)}, u32[]{:S(2)}, u32[]{:S(2)}) async-start(bf16[32,4,32,128]{3,2,1,0:T(8,128)(2,1)} %get-tuple-element.12), calls=%async_computation.2 | async-start | bytes 2097152 | tf_op jit(solution)/shard_map/all_to_all | solution.py:355
  238.4 18.7 %copy-start.20 = (bf16[1024,128]{1,0:T(8,128)(2,1)S(1)}, bf16[1024,128]{1,0:T(8,128)(2,1)}, u32[]{:S(2)}) copy-start(bf16[1024,128]{1,0:T(8,128)(2,1)} %param.19) | copy-start | bytes 786436
  238.4 41.9 %all-gather.11.cloned.1.call-start = ((), (), s32[]{:S(2)}) async-start(), calls=%async_computation.6 | async-start | bytes 1310720 | tf_op jit(solution)/shard_map/all_gather | solution.py:393
  257.5 1.6 copy-start.15
  257.7 22.6 %copy-start.17 = (bf16[512,656]{0,1:T(8,128)(2,1)S(1)}, bf16[512,656]{0,1:T(8,128)(2,1)}, u32[]{:S(2)}) copy-start(bf16[512,656]{0,1:T(8,128)(2,1)} %copy-done.16) | copy-start | bytes 2015236
  285.2 3.4 copy-start.9
  285.2 3.4 copy-start.12
  (11 other events, 12.0 us)
Sparse Core Ops, SparseCore 0:
  11.8 26.4 all-gather.6
  46.3 30.0 reduce-scatter.1
  102.4 48.5 all-gather.12
  154.0 43.1 all-gather.8
  258.7 21.5 all-gather.10

commit v2 on v1

--- a/solution.py
+++ b/solution.py
@@ -17,121 +17,349 @@
     return centre * lax.rsqrt(spread + 1e-05) * gain
 
 
-def gelu_exact(values):
-    return 0.5 * values * (1.0 + jax.scipy.special.erf(values / math.sqrt(2.0)))
-
-
-def gelu_slope(values):
-    cdf = 0.5 * (1.0 + jax.scipy.special.erf(values / math.sqrt(2.0)))
-    return cdf + values * jnp.exp(-0.5 * values * values) / math.sqrt(2.0 * math.pi)
-
-
-def rebuild_kernel(blk_ref, lane_ref, codes_ref, bucket_ref, tab_hbm, out_ref, tab, sem):
-    parts = sem.shape[0]
-    span = tab.shape[1] // parts
-    copies = [
-        pltpu.make_async_copy(
-            tab_hbm.at[:, pl.ds(i * span, span)], tab.at[:, pl.ds(i * span, span)], sem.at[i]
-        )
-        for i in range(parts)
-    ]
-    for copy in copies:
-        copy.start()
-    for copy in copies:
-        copy.wait()
-    passages, dims, toks = out_ref.shape
+def rebuild_passage(p, blk_ref, lane_ref, codes_ref, bucket_ref, tab):
+    dims, toks = tab.shape[0], lane_ref.shape[1]
     lane = lax.broadcasted_iota(jnp.int32, (dims, toks), 1)
     shift = 2 * lax.broadcasted_iota(jnp.int32, (8, toks), 0)
-
-    def passage(p, carry):
-        spot = jnp.broadcast_to(lane_ref[pl.ds(p, 1), :], (dims, toks))
-        base = jnp.zeros((dims, toks), jnp.float32)
-        for j in range(toks):
-            start = pl.multiple_of(blk_ref[p, j] * 128, 128)
-            block = tab[:, pl.ds(start, 128)].astype(jnp.float32)
-            base = jnp.where(lane == j, jnp.take_along_axis(block, spot, axis=1), base)
-        words = codes_ref[p]
-        fields = jnp.concatenate(
-            [
-                jnp.bitwise_and(
-                    jnp.right_shift(jnp.broadcast_to(words[w : w + 1], (8, toks)), shift), 3
-                )
-                for w in range(dims // 8)
-            ],
-            axis=0,
-        )
-        resid = jnp.where(
-            fields < 2,
-            jnp.where(fields == 0, bucket_ref[0], bucket_ref[1]),
-            jnp.where(fields == 2, bucket_ref[2], bucket_ref[3]),
-        )
-        out_ref[p] = (base + resid).astype(jnp.bfloat16)
-        return carry
-
-    lax.fori_loop(0, passages, passage, 0)
-
-
-def rebuild(cent_ids, codes, bucket, table):
+    spot = jnp.broadcast_to(lane_ref[pl.ds(p, 1), :], (dims, toks))
+    base = jnp.zeros((dims, toks), jnp.float32)
+    for j in range(toks):
+        block = tab[:, pl.ds(blk_ref[p, j] * 128, 128)].astype(jnp.float32)
+        base = jnp.where(lane == j, jnp.take_along_axis(block, spot, axis=1), base)
+    words = codes_ref[p]
+    fields = jnp.concatenate(
+        [
+            jnp.bitwise_and(
+                jnp.right_shift(jnp.broadcast_to(words[w : w + 1], (8, toks)), shift), 3
+            )
+            for w in range(dims // 8)
+        ],
+        axis=0,
+    )
+    resid = jnp.where(
+        fields < 2,
+        jnp.where(fields == 0, bucket_ref[0], bucket_ref[1]),
+        jnp.where(fields == 2, bucket_ref[2], bucket_ref[3]),
+    )
+    return (base + resid).astype(jnp.bfloat16)
+
+
+def pair(docs, queries, count):
+    q_len, dim = queries.shape
+    toks = docs.shape[1]
+    spots = lax.broadcasted_iota(jnp.int32, (q_len, toks), 1)
+    values = docs.astype(jnp.float32)
+    scale = lax.rsqrt(jnp.mean(values * values, axis=0, keepdims=True) + 1e-06) / math.sqrt(dim)
+    sims = jnp.dot(queries, docs, preferred_element_type=jnp.float32)
+    raised = jnp.where(spots < count, jnp.exp(64.0 * (sims * scale)), 0.0)
+    total = jnp.sum(raised, axis=1, keepdims=True)
+    score = jnp.sum(jnp.log(total), axis=0, keepdims=True) / 64.0
+    weights = (raised * (scale / total)).astype(jnp.bfloat16)
+    pull = lax.dot_general(
+        weights, docs, (((1,), (1,)), ((), ())), preferred_element_type=jnp.float32
+    )
+    return pull.astype(jnp.bfloat16), score
+
+
+def forward_kernel(
+    side, groups, chunks,
+    states_ref, norm_gain_ref, final_gain_ref, gate_w, up_w, down_w, proj_w,
+    blk_ref, lens_ref, lane_ref, codes_ref, bucket_ref, tables_ref, tab_hbm,
+    rows_ref, slope_ref, gelu_ref, hidden_ref, out_ref, final_ref, proj_ref, pull_ref, score_ref,
+    tab, docs, part, part_own, part_land, asks, asks_smem, queries, pull_out, score_out,
+    tab_sem, asks_sem, rows_send, rows_recv, part_send, part_recv, docs_send, docs_recv,
+    asks_send, asks_recv, query_send, query_recv, pull_send, pull_recv, score_send, score_recv,
+):
+    z, x, core, grp = coords(side)
+    me = (z * side + x) * 2 + core
+    shards = 2 * side * side
+    passages, toks = lane_ref.shape
+    span = passages // chunks
+    tok_rows = states_ref.shape[0]
+    caps, q_len, dim = pull_ref.shape[1:]
+
+    pieces = tab_sem.shape[0]
+    width = tab.shape[1] // pieces
+    table_copies = [
+        pltpu.make_async_copy(
+            tab_hbm.at[:, pl.ds(i * width, width)], tab.at[:, pl.ds(i * width, width)], tab_sem.at[i]
+        )
+        for i in range(pieces)
+    ]
+    for copy in table_copies:
+        copy.start()
+
+    def to(step):
+        dz, dx, dc = step // (2 * side), (step // 2) % side, step % 2
+        return (((z + dz) % side) * side + (x + dx) % side) * 2 + (core + dc) % 2
+
+    def source(step):
+        dz, dx, dc = step // (2 * side), (step // 2) % side, step % 2
+        return (
+            ((z + side - dz) % side) * side + (x + side - dx) % side
+        ) * 2 + (core + 2 - dc) % 2
+
+    barrier = pltpu.get_barrier_semaphore()
+
+    def greet(step, carry):
+        pl.semaphore_signal(barrier, inc=1, device_id=(to(step), grp), device_id_type=MESH)
+        return carry
+
+    lax.fori_loop(1, shards, greet, 0)
+    for step in range(1, groups):
+        pl.semaphore_signal(
+            barrier, inc=1, device_id=(me, (grp + step) % groups), device_id_type=MESH
+        )
+    rows_ref[grp] = layer_norm(states_ref[...].astype(jnp.float32), norm_gain_ref[...]).astype(
+        jnp.bfloat16
+    )
+    pl.semaphore_wait(barrier, shards + groups - 2)
+
+    def along_grp(step, src, dst, send_sem, recv_sem):
+        return pltpu.make_async_remote_copy(
+            src_ref=src, dst_ref=dst, send_sem=send_sem, recv_sem=recv_sem,
+            device_id=(me, (grp + step) % groups), device_id_type=MESH,
+        )
+
+    def came(step):
+        return (grp + groups - step) % groups
+
+    def rows_copy(step, slot):
+        return along_grp(
+            step, rows_ref.at[slot], rows_ref.at[slot], rows_send.at[step], rows_recv.at[step]
+        )
+
+    def part_copy(step):
+        return along_grp(
+            step, part.at[(grp + step) % groups], part_land.at[step - 1],
+            part_send.at[step], part_recv.at[step],
+        )
+
+    def docs_copy(step, chunk, slot):
+        place = docs.at[slot, pl.ds(chunk * span, span)]
+        return along_grp(
+            step, place, place, docs_send.at[chunk, step], docs_recv.at[chunk, step]
+        )
+
+    def along_shard(step, src, dst, send_sems, recv_sems):
+        return pltpu.make_async_remote_copy(
+            src_ref=src, dst_ref=dst, send_sem=send_sems.at[step], recv_sem=recv_sems.at[step],
+            device_id=(to(step), grp), device_id_type=MESH,
+        )
+
+    def asks_copy(step, slot):
+        return along_shard(step, tables_ref.at[to(step)], asks.at[slot], asks_send, asks_recv)
+
+    def query_copy(step, slot):
+        return along_shard(step, queries.at[me], queries.at[slot], query_send, query_recv)
+
+    def back(step, src, dst, send_sems, recv_sems):
+        return pltpu.make_async_remote_copy(
+            src_ref=src, dst_ref=dst, send_sem=send_sems.at[step], recv_sem=recv_sems.at[step],
+            device_id=(source(step), grp), device_id_type=MESH,
+        )
+
+    def pull_copy(step, slot):
+        return back(step, pull_out.at[source(step)], pull_ref.at[slot], pull_send, pull_recv)
+
+    def score_copy(step, slot):
+        return back(step, score_out.at[source(step)], score_ref.at[slot], score_send, score_recv)
+
+    for step in range(1, groups):
+        rows_copy(step, grp).start()
+
+    def ask(step, carry):
+        asks_copy(step, me).start()
+        return carry
+
+    lax.fori_loop(1, shards, ask, 0)
+    asks[me] = tables_ref[me]
+    for copy in table_copies:
+        copy.wait()
+
+    def feed_forward():
+        for step in range(1, groups):
+            rows_copy(step, came(step)).wait_recv()
+
+        def block(r, carry):
+            normed = rows_ref[r]
+            gate = jnp.dot(normed, gate_w[...], preferred_element_type=jnp.float32)
+            up = jnp.dot(normed, up_w[...], preferred_element_type=jnp.float32)
+            cdf = 0.5 * (1.0 + lax.erf(gate * (1.0 / math.sqrt(2.0))))
+            gelu = gate * cdf
+            bell = jnp.exp(-0.5 * gate * gate) * (1.0 / math.sqrt(2.0 * math.pi))
+            slope_ref[r] = ((cdf + gate * bell) * up).astype(jnp.bfloat16)
+            gelu_ref[r] = gelu.astype(jnp.bfloat16)
+            hidden = (gelu * up).astype(jnp.bfloat16)
+            hidden_ref[r] = hidden
+            down = lax.dot_general(
+                hidden, down_w[...], (((1,), (1,)), ((), ())), preferred_element_type=jnp.float32
+            )
+            part[r] = down.astype(jnp.bfloat16)
+
+            @pl.when(r == grp)
+            def _():
+                part_own[...] = down
+
+            return carry
+
+        lax.fori_loop(0, groups, block, 0)
+        for step in range(1, groups):
+            part_copy(step).start()
+
+    def make_queries():
+        out = states_ref[...].astype(jnp.float32) + part_own[...]
+        for step in range(1, groups):
+            part_copy(step).wait_recv()
+            out = out + part_land[step - 1].astype(jnp.float32)
+        out_ref[...] = out
+        final = layer_norm(out, final_gain_ref[...]).astype(jnp.bfloat16)
+        final_ref[...] = final
+        proj = jnp.dot(final, proj_w[...], preferred_element_type=jnp.float32)
+        proj_ref[...] = proj
+        scale = lax.rsqrt(jnp.mean(proj * proj, axis=-1, keepdims=True) + 1e-06) / math.sqrt(dim)
+        queries[me] = (proj * scale).astype(jnp.bfloat16).reshape(tok_rows // q_len, q_len, dim)
+
+        def tell(step, carry):
+            query_copy(step, me).start()
+            return carry
+
+        lax.fori_loop(1, shards, tell, 0)
+
+    def chunk_of(c, carry):
+        def passage(i, carry):
+            p = c * span + i
+            docs[grp, p] = rebuild_passage(p, blk_ref, lane_ref, codes_ref, bucket_ref, tab)
+            return carry
+
+        lax.fori_loop(0, span, passage, 0)
+        for step in range(1, groups):
+            docs_copy(step, c, grp).start()
+        pl.when(c == 0)(feed_forward)
+        pl.when(c == chunks // 2)(make_queries)
+        return carry
+
+    lax.fori_loop(0, chunks, chunk_of, 0)
+
+    def gather_in(step, carry):
+        asks_copy(step, source(step)).wait_recv()
+        query_copy(step, source(step)).wait_recv()
+        return carry
+
+    lax.fori_loop(1, shards, gather_in, 0)
+    to_smem = pltpu.make_async_copy(asks, asks_smem, asks_sem)
+    to_smem.start()
+    to_smem.wait()
+
+    def docs_in(c, carry):
+        for step in range(1, groups):
+            docs_copy(step, c, came(step)).wait_recv()
+        return carry
+
+    lax.fori_loop(0, chunks, docs_in, 0)
+
+    def serve(step, carry):
+        d = source(step)
+        for k in range(caps):
+            p = asks_smem[d, 0, k]
+            raw = jnp.concatenate([docs[g, p] for g in range(groups)], axis=0)
+            pull, score = pair(raw, queries[d, asks_smem[d, 0, caps + k]], lens_ref[p])
+            pull_out[d, k] = pull
+            score_out[d, pl.ds(k, 1), :] = jnp.broadcast_to(score, (1, dim))
+
+        @pl.when(step > 0)
+        def _():
+            pull_copy(step, me).start()
+            score_copy(step, me).start()
+
+        @pl.when(step == 0)
+        def _():
+            pull_ref[me] = pull_out[me]
+            score_ref[me] = score_out[me]
+
+        return carry
+
+    lax.fori_loop(0, shards, serve, 0)
+
+    def finish(step, carry):
+        pull_copy(step, to(step)).wait_recv()
+        score_copy(step, to(step)).wait_recv()
+        asks_copy(step, me).wait_send()
+        query_copy(step, me).wait_send()
+        pull_copy(step, me).wait_send()
+        score_copy(step, me).wait_send()
+        return carry
+
+    lax.fori_loop(1, shards, finish, 0)
+    for step in range(1, groups):
+        rows_copy(step, grp).wait_send()
+        part_copy(step).wait_send()
+
+    def docs_out(c, carry):
+        for step in range(1, groups):
+            docs_copy(step, c, grp).wait_send()
+        return carry
+
+    lax.fori_loop(0, chunks, docs_out, 0)
+
+
+def forward(
+    states, norm_gain, final_gain, w_gate, w_up, w_down_t, w_proj, cent_ids, lens, codes, bucket,
+    tables, table, side, caps, q_len,
+):
+    groups = lax.axis_size("grp")
+    shards = 2 * side * side
+    tok_rows, width = states.shape
+    part = w_gate.shape[1]
+    dim = w_proj.shape[1]
     passages, toks = cent_ids.shape
     dims, count = table.shape
+    chunks = 8
     spread = jnp.broadcast_to(bucket[:, :, None], (4, dims, toks))
+    vmem = pl.BlockSpec(memory_space=pltpu.VMEM)
+    smem = pl.BlockSpec(memory_space=pltpu.SMEM)
+    bf16, f32 = jnp.bfloat16, jnp.float32
+    dma = pltpu.SemaphoreType.DMA
     return pl.pallas_call(
-        rebuild_kernel,
-        out_shape=jax.ShapeDtypeStruct((passages, dims, toks), jnp.bfloat16),
-        in_specs=[
-            pl.BlockSpec(memory_space=pltpu.SMEM),
-            pl.BlockSpec(memory_space=pltpu.VMEM),
-            pl.BlockSpec(memory_space=pltpu.VMEM),
-            pl.BlockSpec(memory_space=pltpu.VMEM),
-            pl.BlockSpec(memory_space=pl.ANY),
-        ],
-        out_specs=pl.BlockSpec(memory_space=pltpu.VMEM),
-        scratch_shapes=[pltpu.VMEM((dims, count), jnp.bfloat16), pltpu.SemaphoreType.DMA((8,))],
-        compiler_params=pltpu.CompilerParams(vmem_limit_bytes=36 << 20),
-        cost_estimate=pl.CostEstimate(flops=0, bytes_accessed=150_000_000, transcendentals=0),
-    )(cent_ids >> 7, cent_ids & 127, codes, spread, table)
-
-
-def pair_kernel(pass_ref, query_ref, lens_ref, docs_ref, q_ref, pull_ref, score_ref):
-    sources, caps, q_len, dim = pull_ref.shape
-    toks = docs_ref.shape[3]
-    spots = lax.broadcasted_iota(jnp.int32, (q_len, toks), 1)
-
-    def source(d, carry):
-        for k in range(caps):
-            p = pass_ref[d, k]
-            raw = jnp.concatenate([docs_ref[g, p] for g in range(docs_ref.shape[0])], axis=0)
-            values = raw.astype(jnp.float32)
-            scale = lax.rsqrt(jnp.mean(values * values, axis=0, keepdims=True) + 1e-06) / math.sqrt(dim)
-            sims = jnp.dot(q_ref[d, query_ref[d, k]], raw, preferred_element_type=jnp.float32)
-            raised = jnp.where(spots < lens_ref[p], jnp.exp(64.0 * (sims * scale)), 0.0)
-            total = jnp.sum(raised, axis=1, keepdims=True)
-            soft = jnp.sum(jnp.log(total), axis=0, keepdims=True) / 64.0
-            weights = (raised * (scale / total)).astype(jnp.bfloat16)
-            pull_ref[d, k] = lax.dot_general(
-                weights, raw, (((1,), (1,)), ((), ())), preferred_element_type=jnp.float32
-            ).astype(jnp.bfloat16)
-            score_ref[d, pl.ds(k, 1), :] = jnp.broadcast_to(soft, (1, dim))
-        return carry
-
-    lax.fori_loop(0, sources, source, 0)
-
-
-def pairs(slot_pass, slot_query, lens, docs, queries):
-    sources, caps = slot_pass.shape
-    q_len, dim = queries.shape[2:]
-    return pl.pallas_call(
-        pair_kernel,
+        functools.partial(forward_kernel, side, groups, chunks),
         out_shape=(
-            jax.ShapeDtypeStruct((sources, caps, q_len, dim), jnp.bfloat16),
-            jax.ShapeDtypeStruct((sources, caps, dim), jnp.float32),
+            jax.ShapeDtypeStruct((groups, tok_rows, width), bf16),
+            jax.ShapeDtypeStruct((groups, tok_rows, part), bf16),
+            jax.ShapeDtypeStruct((groups, tok_rows, part), bf16),
+            jax.ShapeDtypeStruct((groups, tok_rows, part), bf16),
+            jax.ShapeDtypeStruct((tok_rows, width), f32),
+            jax.ShapeDtypeStruct((tok_rows, width), bf16),
+            jax.ShapeDtypeStruct((tok_rows, dim), f32),
+            jax.ShapeDtypeStruct((shards, caps, q_len, dim), bf16),
+            jax.ShapeDtypeStruct((shards, caps, dim), f32),
         ),
-        in_specs=[pl.BlockSpec(memory_space=pltpu.SMEM)] * 3
-        + [pl.BlockSpec(memory_space=pltpu.VMEM)] * 2,
-        out_specs=(pl.BlockSpec(memory_space=pltpu.VMEM),) * 2,
-        compiler_params=pltpu.CompilerParams(vmem_limit_bytes=24 << 20),
-        cost_estimate=pl.CostEstimate(flops=0, bytes_accessed=40_000_000, transcendentals=0),
-    )(slot_pass, slot_query, lens, docs, queries)
+        in_specs=[vmem] * 7 + [smem] * 2 + [vmem] * 4 + [pl.BlockSpec(memory_space=pl.ANY)],
+        out_specs=(vmem,) * 9,
+        scratch_shapes=[
+            pltpu.VMEM((dims, count), bf16),
+            pltpu.VMEM((groups, passages, dims, toks), bf16),
+            pltpu.VMEM((groups, tok_rows, width), bf16),
+            pltpu.VMEM((tok_rows, width), f32),
+            pltpu.VMEM((groups - 1, tok_rows, width), bf16),
+            pltpu.VMEM((shards, 1, 128), jnp.int32),
+            pltpu.SMEM((shards, 1, 128), jnp.int32),
+            pltpu.VMEM((shards, tok_rows // q_len, q_len, dim), bf16),
+            pltpu.VMEM((shards, caps, q_len, dim), bf16),
+            pltpu.VMEM((shards, caps, dim), f32),
+            dma((8,)),
+            dma,
+        ]
+        + [dma((groups,))] * 4
+        + [dma((chunks, groups))] * 2
+        + [dma((shards,))] * 8,
+        compiler_params=pltpu.CompilerParams(
+            collective_id=1, has_side_effects=True, vmem_limit_bytes=56 << 20
+        ),
+        cost_estimate=pl.CostEstimate(flops=0, bytes_accessed=300_000_000, transcendentals=0),
+    )(
+        states, norm_gain, final_gain, w_gate, w_up, w_down_t, w_proj, cent_ids >> 7, lens,
+        cent_ids & 127, codes, spread, tables, table,
+    )
 
 
 def coords(shape):
@@ -320,49 +548,31 @@
     me = lax.axis_index("shard")
 
     flat_ids = negative_ids.reshape(1, -1)
-    column_ids = lax.all_gather(flat_ids, "shard", axis=0, tiled=True)
-    rows = query_states.reshape(tok_rows, width).astype(jnp.float32)
-    normed = layer_norm(rows, norm_gain).astype(jnp.bfloat16)
-    group_rows = lax.all_gather(normed, "grp", axis=0, tiled=True)
-
-    raw = rebuild(centroid_ids, residual_codes, bucket_values, centroids)
-    docs = lax.all_gather(raw, "grp", axis=0)
-
-    gate = jnp.dot(group_rows, w_gate, preferred_element_type=jnp.float32)
-    up = jnp.dot(group_rows, w_up, preferred_element_type=jnp.float32)
-    hidden = (gelu_exact(gate) * up).astype(jnp.bfloat16)
-    out = rows + lax.psum_scatter(
-        lax.dot_general(
-            hidden, w_down_t, (((1,), (1,)), ((), ())), preferred_element_type=jnp.float32
-        ),
-        "grp",
-        scatter_dimension=0,
-        tiled=True,
-    )
-    final = layer_norm(out, final_gain).astype(jnp.bfloat16)
-    proj = jnp.dot(final, w_proj, preferred_element_type=jnp.float32)
+    owner = lax.broadcasted_iota(jnp.int32, (shards, 1), 0)
+    places = lax.broadcasted_iota(jnp.int32, (1, 1, q_dev * cands), 2)
+    sent = slots(flat_ids // local_pass == owner, caps)
+    place = jnp.sum(jnp.where(sent, places, 0), axis=2)
+    asked = jnp.sum(jnp.where(sent, (flat_ids % local_pass)[:, None, :], 0), axis=2)
+    tables = jnp.concatenate(
+        [asked, place // cands, jnp.zeros((shards, 128 - 2 * caps), jnp.int32)], axis=1
+    ).reshape(shards, 1, 128)
+    lens = lax.dynamic_slice(passage_lens, (me * local_pass,), (local_pass,))
+    states = query_states.reshape(tok_rows, width)
+    group_rows, slope, gelu, hidden, out, final, proj, pull, score = forward(
+        states, norm_gain.reshape(1, -1), final_gain.reshape(1, -1), w_gate, w_up, w_down_t, w_proj,
+        centroid_ids, lens, residual_codes, bucket_values, tables, centroids, side, caps, q_len,
+    )
+    group_rows = group_rows.reshape(groups * tok_rows, width)
+    slope, gelu, hidden = (v.reshape(groups * tok_rows, -1) for v in (slope, gelu, hidden))
     length = lax.rsqrt(jnp.mean(proj * proj, axis=-1, keepdims=True) + 1e-06)
     scale = length / math.sqrt(dim)
-    queries = (proj * scale).astype(jnp.bfloat16).reshape(1, q_dev, q_len, dim)
-    column_queries = lax.all_gather(queries, "shard", axis=0, tiled=True)
-
-    asked = slots(column_ids // local_pass == me, caps)
-    places = lax.broadcasted_iota(jnp.int32, (1, 1, q_dev * cands), 2)
-    slot_pass = jnp.sum(jnp.where(asked, (column_ids % local_pass)[:, None, :], 0), axis=2)
-    slot_query = jnp.sum(jnp.where(asked, places // cands, 0), axis=2)
-    lens = lax.dynamic_slice(passage_lens, (me * local_pass,), (local_pass,))
-    pull, score = pairs(slot_pass, slot_query, lens, docs, column_queries)
-    pull = lax.all_to_all(pull, "shard", split_axis=0, concat_axis=0, tiled=True)
-    score = lax.all_to_all(score[:, :, :1], "shard", split_axis=0, concat_axis=0, tiled=True)
-
-    owner = lax.broadcasted_iota(jnp.int32, (shards, 1), 0)
-    sent = slots(flat_ids // local_pass == owner, caps)
+
     filled = jnp.any(sent, axis=2).reshape(1, -1)
-    place = jnp.sum(jnp.where(sent, places, 0), axis=2).reshape(1, -1)
+    place = place.reshape(1, -1)
     query = lax.broadcasted_iota(jnp.int32, (q_dev, 1), 0)
     mine = filled & (place // cands == query)
     first = mine & (place % cands == 0)
-    scores = 10.0 * score.reshape(1, -1)
+    scores = 10.0 * score[:, :, 0].reshape(1, -1)
     top = jnp.max(jnp.where(mine, scores, -jnp.inf), axis=1, keepdims=True)
     raised = jnp.where(mine, jnp.exp(scores - top), 0.0)
     total = jnp.sum(raised, axis=1, keepdims=True)
@@ -392,8 +602,8 @@
     dout_b = dout.astype(jnp.bfloat16)
     group_grad = lax.all_gather(dout_b, "grp", axis=0, tiled=True)
     dhid = jnp.dot(group_grad, w_down_t, preferred_element_type=jnp.float32)
-    dgate = (dhid * up * gelu_slope(gate)).astype(jnp.bfloat16)
-    dup = (dhid * gelu_exact(gate)).astype(jnp.bfloat16)
+    dgate = (dhid * slope.astype(jnp.float32)).astype(jnp.bfloat16)
+    dup = (dhid * gelu.astype(jnp.float32)).astype(jnp.bfloat16)
     term_gate = lax.dot_general(group_rows, dgate, contract, preferred_element_type=jnp.float32)
     term_up = lax.dot_general(group_rows, dup, contract, preferred_element_type=jnp.float32)
     term_down = lax.dot_general(group_grad, hidden, contract, preferred_element_type=jnp.float32)

time: 361 us -> 238 us (0.66)
  waiting for transfers between devices: 135 us -> 16.2 us
  Pallas kernels: 115 us -> 156 us
  blocking collectives: 21.6 us -> 0 us
  starting transfers between devices: 9.51 us -> 0.04 us
  matrix products: 20.6 us -> 14.5 us
  other arithmetic: 14.1 us -> 8.64 us
    all_gather x3 -> x0, waiting for transfers between devices: 94.2 us -> none  [the longest x1 46.2 us: local(): column_queries = lax.all_gather(queries, 'shard', axis=0, tiled=True)]
    pallas_call x2 -> x1, Pallas kernels: 69.8 us -> 111 us  [forward(): pl.pallas_call(functools.partial(forward_kernel, side, groups, chunks), o...]
    all_gather x1 -> x0, blocking collectives: 21.6 us -> none  [local(): column_ids = lax.all_gather(flat_ids, 'shard', axis=0, tiled=True)]
    all_to_all x2 -> x0, waiting for transfers between devices: 19.7 us -> none  [the longest x1 13.5 us: local(): lax.all_to_all(pull, 'shard', split_axis=0, concat_axis=0, tiled=True)]
    all_to_all x2 -> x0, starting transfers between devices: 9.13 us -> none  [the longest x1 5.2 us: local(): lax.all_to_all(score[:, :, :1], 'shard', split_axis=0, concat_axis=0, til...]
    dot_general x4 -> x0, matrix products: 7.32 us -> none  [the longest x1 2.63 us: local(): gate = jnp.dot(group_rows, w_gate, preferred_element_type=jnp.float32)]
    unnamed x61 -> x37, local copies, waits for them, and re-layouts: 17.4 us -> 11.8 us
    all_gather x1, waiting for transfers between devices: 20.9 us -> 16.2 us  [local(): group_grad = lax.all_gather(dout_b, 'grp', axis=0, tiled=True)]
  transfers between devices with their start and end apart: 7 -> 1, of which waited for: 6 -> 1; matrix products, arithmetic and copies ran while one was open for 3% -> 3% of each run, Pallas kernels for 14% -> 0%
where the time goes in v2:
time: 238 us; the launch traced here: 235 us
  Pallas kernels  156 us (66%)
  local copies, waits for them, and re-layouts  24.4 us (10%)
  waiting for transfers between devices  16.2 us (7%)
  matrix products  14.5 us (6%)
  between operations  14.3 us (6%)
  other arithmetic  8.64 us (4%)
    pallas_call x1, Pallas kernels, forward(): pl.pallas_call(functools.partial(forward_kernel, side, groups, chunks), o...  111 us
    pallas_call x1, Pallas kernels, scatter_sums(): pl.pallas_call(functools.partial(scatter_kernel, side, groups), out_shape...  45.1 us
    all_gather x1, waiting for transfers between devices, local(): group_grad = lax.all_gather(dout_b, 'grp', axis=0, tiled=True)  16.2 us
    unnamed x37, local copies, waits for them, and re-layouts  11.8 us
  transfers between devices with their start and end apart: 1, of which 1 were waited for; matrix products, arithmetic and copies ran while one was open for 3% of the time, Pallas kernels for 0%

profile of v2, /device:TPU:0, one launch (start us, length us, event | category | flops | bytes accessed | tf_op | source)
XLA Modules:
  0.0 234.6 jit_solution(14179716501538756174)
XLA Ops:
  9.2 1.5 broadcast_and_fusion
  10.7 2.7 %copy.41.gate_w = bf16[1024,656]{1,0:T(8,128)(2,1)} copy(bf16[1024,656]{0,1:T(8,128)(2,1)} %param.16) | data formatting | bytes 2686976 | tf_op args[3]
  13.3 1.6 copy.42.up_w
  14.9 1.5 copy.43.down_w
  16.5 1.3 dynamic_slice.3.lens_ref
  19.1 111.4 %shard_map.164 = (bf16[4,128,1024]{2,1,0:T(8,128)(2,1)}, bf16[4,128,656]{2,1,0:T(8,128)(2,1)}, bf16[4,128,656]{2,1,0:T(8,128)(2,1)}, bf16[4,128,656]{2,1,0:T(8,1...) custom-call(bf16[128,1024]{1,0:T(8,128)(2,1)} %bitcast.38, ...), custom_call_target="tpu_custom_call" | custom-call | bytes 300000000 | tf_op jit(solution)/shard_map/pallas_call | solution.py:323
  131.7 1.2 reduce_sum.104
  133.3 1.6 fusion
  136.7 1.6 bitcast_convert_fusion
  138.3 1.5 copy.46
  139.8 1.5 copy.44
  141.9 1.1 fusion.21
  143.0 16.2 %all-gather.2.cloned.1.call-done = bf16[512,1024]{1,0:T(8,128)(2,1)} async-done(((bf16[128,1024]{1,0:T(8,128)(2,1)}), bf16[512,1024]{1,0:T(8,128)(2,1)}) %all-gather.2.cloned.1.call-update) | async-done | bytes 1048592 | tf_op jit(solution)/shard_map/all_gather | solution.py:603
  159.1 3.2 %convolution_convert_fusion = bf16[1024,656]{0,1:T(8,128)(2,1)} fusion(bf16[512,1024]{1,0:T(8,128)(2,1)} %all-gather.2.cloned.1.call-done, bf16[512,656]{1,0:T(8,128)(2,1)S(1)} %bitcast.42), kind=kOutput, calls=%fused_computation | convolution fusion | flops 688537600 | bytes 3063808 | tf_op jit(solution)/shard_map/dot_general | solution.py:609
  162.4 1.8 copy.48
  164.2 2.3 fusion.20
  166.4 1.1 copy-done.3
  167.5 2.0 convolution_convert_fusion.1
  169.5 1.7 copy.47
  171.1 4.0 %convolution_convert_fusion.2 = bf16[1024,656]{0,1:T(8,128)(2,1)} fusion(bf16[512,1024]{1,0:T(8,128)(2,1)} %bitcast.35, f32[512,656]{0,1:T(8,128)} %copy-done.3, f32[512,656]{0,1:T(8,128)} %copy.44), kind=kOutput, calls=%fused_computation.2 | convolution fusion | flops 689209344 | bytes 5079040 | tf_op jit(solution)/shard_map/dot_general | solution.py:607
  175.1 2.6 %copy.45 = bf16[1024,656]{1,0:T(8,128)(2,1)} copy(bf16[1024,656]{0,1:T(8,128)(2,1)} %convolution_convert_fusion.2) | data formatting | bytes 2686976 | tf_op jit(solution)/shard_map/convert_element_type | solution.py:611
  177.7 1.4 copy-done
  179.1 1.0 copy-done.1
  180.1 45.1 %shard_map.165 = (f32[32,656]{1,0:T(8,128)S(1)}, f32[32,656]{1,0:T(8,128)S(1)}, f32[32,656]{1,0:T(8,128)S(1)}, f32[8,128]{1,0:T(8,128)S(1)}) custom-call(bf16[16,2,32,656]{3,2,1,0:T(8,128)(2,1)S(1)} %bitcast.33, bf16[16,2,32,656]{3,2,1,0:T(8,128)(2,1)S(1)} %bitcast.32, bf16[16,2,32,656]{3,2,1,0:T(8,128)(2,1)S(1)} %bitcast.31, f32[16,2,32,128]{3,2,1,0:T(8,128)S(1)} %bitcast.34), custom_call_target="tpu_custom_call" | custom-call | bytes 60000000 | tf_op jit(solution)/shard_map/pallas_call | solution.py:480
  (68 shorter events, 9.7 us)
Async XLA Ops:
  7.2 152.0 %all-gather.2.cloned.1.call-start = ((), (), s32[]{:S(2)}) async-start(), calls=%async_computation | async-start | bytes 1310720 | tf_op jit(solution)/shard_map/all_gather | solution.py:603
  10.7 2.7 %copy-start.6 = (bf16[1024,656]{0,1:T(8,128)(2,1)S(1)}, bf16[1024,656]{0,1:T(8,128)(2,1)}, u32[]{:S(2)}) copy-start(bf16[1024,656]{0,1:T(8,128)(2,1)} %param.17) | copy-start | bytes 4030468
  13.3 1.6 copy-start.7
  14.9 3.5 %copy-start.13 = (f32[4,32]{1,0:T(4,128)S(1)}, f32[4,32]{1,0:T(4,128)}, u32[]{:S(2)}) copy-start(f32[4,32]{1,0:T(4,128)} %param.21) | copy-start | bytes 1540
  130.5 4.4 %copy-start.11 = (f32[128,128]{1,0:T(8,128)S(1)}, f32[128,128]{1,0:T(8,128)}, u32[]{:S(2)}) copy-start(f32[128,128]{1,0:T(8,128)} %get-tuple-element.20) | copy-start | bytes 196612
  130.5 4.7 %copy-start.4 = (f32[128,1024]{1,0:T(8,128)S(1)}, f32[128,1024]{1,0:T(8,128)}, u32[]{:S(2)}) copy-start(f32[128,1024]{1,0:T(8,128)} %get-tuple-element.22) | copy-start | bytes 1572868
  130.6 4.7 %copy-start.9 = (bf16[1024,128]{1,0:T(8,128)(2,1)S(1)}, bf16[1024,128]{1,0:T(8,128)(2,1)}, u32[]{:S(2)}) copy-start(bf16[1024,128]{1,0:T(8,128)(2,1)} %proj_w.1) | copy-start | bytes 786436
  130.6 4.7 %copy-start.12 = (f32[1024]{0:T(1024)S(1)}, f32[1024]{0:T(1024)}, u32[]{:S(2)}) copy-start(f32[1024]{0:T(1024)} %param.15) | copy-start | bytes 12292
  139.8 2.0 copy-start.10
  139.8 19.3 %copy-start.14 = (bf16[4,128,656]{2,1,0:T(8,128)(2,1)S(1)}, bf16[4,128,656]{2,1,0:T(8,128)(2,1)}, u32[]{:S(2)}) copy-start(bf16[4,128,656]{2,1,0:T(8,128)(2,1)} %get-tuple-element.25) | copy-start | bytes 2015236
  162.3 1.8 copy-start.8
  164.1 3.4 %copy-start.2 = (f32[512,656]{0,1:T(8,128)S(1)}, f32[512,656]{0,1:T(8,128)}, u32[]{:S(2)}) copy-start(f32[512,656]{0,1:T(8,128)} %copy.46) | copy-start | bytes 4030468
  164.2 3.4 %copy-start.5 = (bf16[4,128,1024]{2,1,0:T(8,128)(2,1)S(1)}, bf16[4,128,1024]{2,1,0:T(8,128)(2,1)}, u32[]{:S(2)}) copy-start(bf16[4,128,1024]{2,1,0:T(8,128)(2,1)} %get-tuple-element.19) | copy-start | bytes 3145732
  166.4 1.1 copy-start.3
  177.7 1.4 copy-start
  179.1 1.0 copy-start.1
Sparse Core Ops, SparseCore 0:
  136.8 22.2 all-gather.1

commit v3 on v2

v3 whole, which is shorter than its diff:
```python
import functools
import math

import jax
import jax.numpy as jnp
from jax import lax
from jax.experimental import pallas as pl
from jax.experimental.pallas import tpu as pltpu
from jax.sharding import PartitionSpec as P

MESH = pl.DeviceIdType.MESH


def layer_norm(rows, gain):
    centre = rows - jnp.mean(rows, axis=-1, keepdims=True)
    spread = jnp.mean(centre * centre, axis=-1, keepdims=True)
    return centre * lax.rsqrt(spread + 1e-05) * gain


def rebuild_passage(p, blk_ref, lane_ref, codes_ref, bucket_ref, tab):
    dims, toks = tab.shape[0], lane_ref.shape[1]
    lane = lax.broadcasted_iota(jnp.int32, (dims, toks), 1)
    shift = 2 * lax.broadcasted_iota(jnp.int32, (8, toks), 0)
    spot = jnp.broadcast_to(lane_ref[pl.ds(p, 1), :], (dims, toks))
    base = jnp.zeros((dims, toks), jnp.float32)
    for j in range(toks):
        block = tab[:, pl.ds(blk_ref[p, j] * 128, 128)].astype(jnp.float32)
        base = jnp.where(lane == j, jnp.take_along_axis(block, spot, axis=1), base)
    words = codes_ref[p]
    fields = jnp.concatenate(
        [
            jnp.bitwise_and(
                jnp.right_shift(jnp.broadcast_to(words[w : w + 1], (8, toks)), shift), 3
            )
            for w in range(dims // 8)
        ],
        axis=0,
    )
    resid = jnp.where(
        fields < 2,
        jnp.where(fields == 0, bucket_ref[0], bucket_ref[1]),
        jnp.where(fields == 2, bucket_ref[2], bucket_ref[3]),
    )
    return (base + resid).astype(jnp.bfloat16)


def dot_t(left, right):
    return lax.dot_general(
        left, right, (((1,), (1,)), ((), ())), preferred_element_type=jnp.float32
    )


def pair(docs, queries, count):
    q_len, dim = queries.shape
    toks = docs.shape[1]
    spots = lax.broadcasted_iota(jnp.int32, (q_len, toks), 1)
    values = docs.astype(jnp.float32)
    scale = lax.rsqrt(jnp.mean(values * values, axis=0, keepdims=True) + 1e-06) / math.sqrt(dim)
    sims = jnp.dot(queries, docs, preferred_element_type=jnp.float32)
    raised = jnp.where(spots < count, jnp.exp(64.0 * (sims * scale)), 0.0)
    total = jnp.sum(raised, axis=1, keepdims=True)
    score = jnp.sum(jnp.log(total), axis=0, keepdims=True) / 64.0
    pull = dot_t((raised * (scale / total)).astype(jnp.bfloat16), docs)
    return pull.astype(jnp.bfloat16), score


def step_kernel(
    side, groups, chunks,
    states_ref, norm_gain_ref, final_gain_ref, gate_w, up_w, down_w, proj_w,
    blk_ref, lens_ref, lane_ref, codes_ref, bucket_ref, tables_ref, which_ref, tab_hbm,
    loss_ref, gate_out, up_out, down_out, proj_out,
    tab, docs, rows_ref, slope_ref, gelu_ref, hidden_ref, part, part_own, part_land, out_ref,
    final_t, proj_ref, asks, asks_smem, queries, pull_out, score_out, pull_ref, score_ref,
    weights, douts, rows_t, douts_t, dgate, dup, first, twin, held, land,
    proj_term, twin_proj, held_proj, land_proj, rows_sum, land_grp,
    tab_sem, asks_sem, rows_send, rows_recv, part_send, part_recv, dout_send, dout_recv,
    grp_send, grp_recv, docs_send, docs_recv,
    asks_send, asks_recv, query_send, query_recv, pull_send, pull_recv, score_send, score_recv,
    twin_send, twin_recv, chip_send, chip_recv,
):
    z, x, core, grp = coords(side)
    me = (z * side + x) * 2 + core
    shards = 2 * side * side
    passages, toks = lane_ref.shape
    span = passages // chunks
    tok_rows = states_ref.shape[0]
    caps, q_len, dim = pull_ref.shape[1:]

    pieces = tab_sem.shape[0]
    width = tab.shape[1] // pieces
    table_copies = [
        pltpu.make_async_copy(
            tab_hbm.at[:, pl.ds(i * width, width)], tab.at[:, pl.ds(i * width, width)], tab_sem.at[i]
        )
        for i in range(pieces)
    ]
    for copy in table_copies:
        copy.start()

    def to(step):
        dz, dx, dc = step // (2 * side), (step // 2) % side, step % 2
        return (((z + dz) % side) * side + (x + dx) % side) * 2 + (core + dc) % 2

    def source(step):
        dz, dx, dc = step // (2 * side), (step // 2) % side, step % 2
        return (
            ((z + side - dz) % side) * side + (x + side - dx) % side
        ) * 2 + (core + 2 - dc) % 2

    barrier = pltpu.get_barrier_semaphore()

    def greet(step, carry):
        pl.semaphore_signal(barrier, inc=1, device_id=(to(step), grp), device_id_type=MESH)
        return carry

    lax.fori_loop(1, shards, greet, 0)
    for step in range(1, groups):
        pl.semaphore_signal(
            barrier, inc=1, device_id=(me, (grp + step) % groups), device_id_type=MESH
        )
    rows_ref[grp] = layer_norm(states_ref[...].astype(jnp.float32), norm_gain_ref[...]).astype(
        jnp.bfloat16
    )
    pl.semaphore_wait(barrier, shards + groups - 2)

    def along_grp(step, src, dst, send_sem, recv_sem):
        return pltpu.make_async_remote_copy(
            src_ref=src, dst_ref=dst, send_sem=send_sem, recv_sem=recv_sem,
            device_id=(me, (grp + step) % groups), device_id_type=MESH,
        )

    def came(step):
        return (grp + groups - step) % groups

    def rows_copy(step, slot):
        return along_grp(
            step, rows_ref.at[slot], rows_ref.at[slot], rows_send.at[step], rows_recv.at[step]
        )

    def part_copy(step):
        return along_grp(
            step, part.at[(grp + step) % groups], part_land.at[step - 1],
            part_send.at[step], part_recv.at[step],
        )

    def docs_copy(step, chunk, slot):
        place = docs.at[slot, pl.ds(chunk * span, span)]
        return along_grp(
            step, place, place, docs_send.at[chunk, step], docs_recv.at[chunk, step]
        )

    def along_shard(step, src, dst, send_sems, recv_sems):
        return pltpu.make_async_remote_copy(
            src_ref=src, dst_ref=dst, send_sem=send_sems.at[step], recv_sem=recv_sems.at[step],
            device_id=(to(step), grp), device_id_type=MESH,
        )

    def asks_copy(step, slot):
        return along_shard(step, tables_ref.at[to(step)], asks.at[slot], asks_send, asks_recv)

    def query_copy(step, slot):
        return along_shard(step, queries.at[me], queries.at[slot], query_send, query_recv)

    def back(step, src, dst, send_sems, recv_sems):
        return pltpu.make_async_remote_copy(
            src_ref=src, dst_ref=dst, send_sem=send_sems.at[step], recv_sem=recv_sems.at[step],
            device_id=(source(step), grp), device_id_type=MESH,
        )

    def pull_copy(step, slot):
        return back(step, pull_out.at[source(step)], pull_ref.at[slot], pull_send, pull_recv)

    def score_copy(step, slot):
        return back(step, score_out.at[source(step)], score_ref.at[slot], score_send, score_recv)

    for step in range(1, groups):
        rows_copy(step, grp).start()

    def ask(step, carry):
        asks_copy(step, me).start()
        return carry

    lax.fori_loop(1, shards, ask, 0)
    asks[me] = tables_ref[me]
    for copy in table_copies:
        copy.wait()

    def feed_forward():
        for step in range(1, groups):
            rows_copy(step, came(step)).wait_recv()

        def block(r, carry):
            normed = rows_ref[r]
            gate = dot_t(normed, gate_w[...])
            up = dot_t(normed, up_w[...])
            cdf = 0.5 * (1.0 + lax.erf(gate * (1.0 / math.sqrt(2.0))))
            gelu = gate * cdf
            bell = jnp.exp(-0.5 * gate * gate) * (1.0 / math.sqrt(2.0 * math.pi))
            slope_ref[r] = ((cdf + gate * bell) * up).astype(jnp.bfloat16)
            gelu_ref[r] = gelu.astype(jnp.bfloat16)
            hidden = (gelu * up).astype(jnp.bfloat16)
            hidden_ref[r] = hidden
            down = jnp.dot(hidden, down_w[...], preferred_element_type=jnp.float32)
            part[r] = down.astype(jnp.bfloat16)

            @pl.when(r == grp)
            def _():
                part_own[...] = down

            return carry

        lax.fori_loop(0, groups, block, 0)
        for step in range(1, groups):
            part_copy(step).start()

    def make_queries():
        out = states_ref[...].astype(jnp.float32) + part_own[...]
        for step in range(1, groups):
            part_copy(step).wait_recv()
            out = out + part_land[step - 1].astype(jnp.float32)
        out_ref[...] = out
        final = layer_norm(out, final_gain_ref[...]).astype(jnp.bfloat16)
        final_t[...] = final.T
        proj = jnp.dot(final, proj_w[...], preferred_element_type=jnp.float32)
        proj_ref[...] = proj
        scale = lax.rsqrt(jnp.mean(proj * proj, axis=-1, keepdims=True) + 1e-06) / math.sqrt(dim)
        queries[me] = (proj * scale).astype(jnp.bfloat16).reshape(tok_rows // q_len, q_len, dim)

        def tell(step, carry):
            query_copy(step, me).start()
            return carry

        lax.fori_loop(1, shards, tell, 0)

    def chunk_of(c, carry):
        def passage(i, carry):
            p = c * span + i
            docs[grp, p] = rebuild_passage(p, blk_ref, lane_ref, codes_ref, bucket_ref, tab)
            return carry

        lax.fori_loop(0, span, passage, 0)
        for step in range(1, groups):
            docs_copy(step, c, grp).start()
        pl.when(c == 0)(feed_forward)
        pl.when(c == chunks // 2)(make_queries)
        return carry

    lax.fori_loop(0, chunks, chunk_of, 0)

    def gather_in(step, carry):
        asks_copy(step, source(step)).wait_recv()
        query_copy(step, source(step)).wait_recv()
        return carry

    lax.fori_loop(1, shards, gather_in, 0)
    to_smem = pltpu.make_async_copy(asks, asks_smem, asks_sem)
    to_smem.start()
    to_smem.wait()

    def docs_in(c, carry):
        for step in range(1, groups):
            docs_copy(step, c, came(step)).wait_recv()
        return carry

    lax.fori_loop(0, chunks, docs_in, 0)

    def serve(step, carry):
        d = source(step)
        rows = []
        for k in range(caps):
            p = asks_smem[d, 0, k]
            raw = jnp.concatenate([docs[g, p] for g in range(groups)], axis=0)
            pull, score = pair(raw, queries[d, asks_smem[d, 0, caps + k]], lens_ref[p])
            pull_out[d, k] = pull
            rows.append(jnp.broadcast_to(score, (1, dim)))
        score_out[d] = jnp.concatenate(rows + [jnp.zeros((8 - caps, dim), jnp.float32)], axis=0)

        @pl.when(step > 0)
        def _():
            pull_copy(step, me).start()
            score_copy(step, me).start()

        @pl.when(step == 0)
        def _():
            pull_ref[me] = pull_out[me]
            score_ref[me] = score_out[me]

        return carry

    lax.fori_loop(0, shards, serve, 0)

    for r in range(groups):
        turned = rows_ref[r].T.reshape(side * side, 2, rows_t.shape[2], tok_rows)
        rows_t[:, :, :, r * tok_rows : (r + 1) * tok_rows] = turned

    def finish(step, carry):
        pull_copy(step, to(step)).wait_recv()
        score_copy(step, to(step)).wait_recv()
        return carry

    lax.fori_loop(1, shards, finish, 0)

    which = which_ref[...]
    scores = 10.0 * score_ref[...].reshape(which.shape)
    top = jnp.max(jnp.where(which > 0, scores, -1e30), axis=0, keepdims=True)
    raised = jnp.where(which > 0, jnp.exp(scores - top), 0.0)
    total = jnp.sum(raised, axis=0, keepdims=True)
    chosen = jnp.sum(jnp.where(which == 2, scores, 0.0), axis=0, keepdims=True)
    loss_ref[...] = jnp.broadcast_to(top + jnp.log(total) - chosen, loss_ref.shape)
    spread = 10.0 * (raised / total - jnp.where(which == 2, 1.0, 0.0))
    q_dev = tok_rows // q_len
    for q in range(q_dev):
        weights[q] = jnp.broadcast_to(spread[:, q : q + 1], spread.shape).reshape(
            weights.shape[1:]
        )

    def gather_pull(s, sums):
        sums = list(sums)
        for k in range(caps):
            term = pull_ref[s, k].astype(jnp.float32)
            for q in range(q_dev):
                sums[q] = sums[q] + weights[q, s, k : k + 1, :] * term
        return tuple(sums)

    zero = jnp.zeros((q_len, dim), jnp.float32)
    sums = lax.fori_loop(0, shards, gather_pull, (zero,) * q_dev)
    dqueries = jnp.concatenate(sums, axis=0).astype(jnp.bfloat16).astype(jnp.float32)
    proj = proj_ref[...]
    length = lax.rsqrt(jnp.mean(proj * proj, axis=-1, keepdims=True) + 1e-06)
    along = jnp.mean(dqueries * proj, axis=-1, keepdims=True)
    dproj = (
        (length / math.sqrt(dim)) * (dqueries - proj * (length * length * along))
    ).astype(jnp.bfloat16)

    dfinal = dot_t(dproj, proj_w[...]) * final_gain_ref[...]
    out = out_ref[...]
    centre = out - jnp.mean(out, axis=-1, keepdims=True)
    inverse = lax.rsqrt(jnp.mean(centre * centre, axis=-1, keepdims=True) + 1e-05)
    unit = centre * inverse
    dout = inverse * (
        dfinal
        - jnp.mean(dfinal, axis=-1, keepdims=True)
        - unit * jnp.mean(dfinal * unit, axis=-1, keepdims=True)
    )
    douts[grp] = dout.astype(jnp.bfloat16)

    def dout_copy(step, slot):
        return along_grp(
            step, douts.at[slot], douts.at[slot], dout_send.at[step], dout_recv.at[step]
        )

    for step in range(1, groups):
        dout_copy(step, grp).start()

    chips = side * side
    chip = me // 2
    block = rows_t.shape[2]

    def swap(src, dst, i):
        return pltpu.make_async_remote_copy(
            src_ref=src, dst_ref=dst, send_sem=twin_send.at[i], recv_sem=twin_recv.at[i],
            device_id=(chip * 2 + 1 - core, grp), device_id_type=MESH,
        )

    def chip_to(step):
        return ((z + step // side) % side) * side + (x + step % side) % side

    def chip_copy(step, src, dst, kind):
        return pltpu.make_async_remote_copy(
            src_ref=src.at[chip_to(step)], dst_ref=dst.at[step - 1],
            send_sem=chip_send.at[kind, step - 1], recv_sem=chip_recv.at[kind, step - 1],
            device_id=(chip_to(step) * 2 + core, grp), device_id_type=MESH,
        )

    proj_term[...] = jnp.dot(
        final_t[...], dproj, preferred_element_type=jnp.float32
    ).reshape(proj_term.shape)
    proj_swap = swap(proj_term.at[:, 1 - core], twin_proj, side)
    proj_swap.start()

    def spread_back(i, carry):
        @pl.when(i > 0)
        def _():
            dout_copy(i, (grp + groups - i) % groups).wait_recv()

        r = (grp + groups - i) % groups
        dhid = dot_t(douts[r], down_w[...])
        dgate[r] = (dhid * slope_ref[r].astype(jnp.float32)).astype(jnp.bfloat16)
        dup[r] = (dhid * gelu_ref[r].astype(jnp.float32)).astype(jnp.bfloat16)
        return carry

    lax.fori_loop(0, groups, spread_back, 0)
    for r in range(groups):
        turned = douts[r].T.reshape(chips, 2, block, tok_rows)
        douts_t[:, :, :, r * tok_rows : (r + 1) * tok_rows] = turned

    proj_swap.wait_recv()

    def add_proj(c, carry):
        held_proj[c] = proj_term[c, core] + twin_proj[c]
        return carry

    lax.fori_loop(0, chips, add_proj, 0)

    def send_proj(step, carry):
        chip_copy(step, held_proj, land_proj, 0).start()
        return carry

    lax.fori_loop(1, chips, send_proj, 0)

    tokens = groups * tok_rows

    def term(i, start, half):
        left = (rows_t, rows_t, douts_t)[i]
        right = (dgate, dup, hidden_ref)[i]
        return jnp.dot(
            left[pl.ds(start, side), half].reshape(side * block, tokens),
            right[...].reshape(tokens, right.shape[2]),
            preferred_element_type=jnp.float32,
        ).reshape(side, block, right.shape[2])

    def band(i):
        return ((z + 1 + i) % side) * side

    def swap_copy(i):
        return swap(first.at[pl.ds(band(i), side)], twin.at[pl.ds(band(i), side)], i)

    def give(i, carry):
        for n in range(3):
            first[pl.ds(band(i), side), n] = term(n, band(i), 1 - core).astype(jnp.bfloat16)
        swap_copy(i).start()
        return carry

    lax.fori_loop(0, side, give, 0)

    def keep(i, carry):
        swap_copy(i).wait_recv()
        for n in range(3):
            held[pl.ds(band(i), side), n] = (
                term(n, band(i), core) + twin[pl.ds(band(i), side), n].astype(jnp.float32)
            ).astype(jnp.bfloat16)
        for dx in range(side):
            step = ((1 + i) % side) * side + dx

            @pl.when(step > 0)
            def _():
                chip_copy(step, held, land, 1).start()

        return carry

    lax.fori_loop(0, side, keep, 0)

    def proj_in(step, total):
        chip_copy(step, held_proj, land_proj, 0).wait_recv()
        return total + land_proj[step - 1]

    rows_sum[...] = lax.fori_loop(1, chips, proj_in, held_proj[chip]).reshape(rows_sum.shape)

    def sum_copy(step):
        return along_grp(
            step, rows_sum.at[(grp + step) % groups], land_grp.at[step - 1],
            grp_send.at[step], grp_recv.at[step],
        )

    for step in range(1, groups):
        sum_copy(step).start()
    mine = rows_sum[grp]
    for step in range(1, groups):
        sum_copy(step).wait_recv()
        mine = mine + land_grp[step - 1]
    proj_out[...] = mine

    for n, ref in enumerate((gate_out, up_out, down_out)):
        ref[...] = held[chip, n].astype(jnp.float32)

    def sum_in(i, carry):
        for dx in range(side):
            step = ((1 + i) % side) * side + dx

            @pl.when(step > 0)
            def _():
                chip_copy(step, held, land, 1).wait_recv()
                for n, ref in enumerate((gate_out, up_out, down_out)):
                    ref[...] += land[step - 1, n].astype(jnp.float32)

        return carry

    lax.fori_loop(0, side, sum_in, 0)

    def sent(step, carry):
        asks_copy(step, me).wait_send()
        query_copy(step, me).wait_send()
        pull_copy(step, me).wait_send()
        score_copy(step, me).wait_send()
        return carry

    lax.fori_loop(1, shards, sent, 0)
    for step in range(1, groups):
        rows_copy(step, grp).wait_send()
        part_copy(step).wait_send()
        dout_copy(step, grp).wait_send()
        sum_copy(step).wait_send()

    def docs_out(c, carry):
        for step in range(1, groups):
            docs_copy(step, c, grp).wait_send()
        return carry

    lax.fori_loop(0, chunks, docs_out, 0)
    proj_swap.wait_send()

    def swapped(i, carry):
        swap_copy(i).wait_send()
        return carry

    lax.fori_loop(0, side, swapped, 0)

    def chips_out(step, carry):
        chip_copy(step, held_proj, land_proj, 0).wait_send()
        chip_copy(step, held, land, 1).wait_send()
        return carry

    lax.fori_loop(1, chips, chips_out, 0)


def step_call(
    states, norm_gain, final_gain, w_gate, w_up, w_down_t, w_proj, cent_ids, lens, codes, bucket,
    tables, which, table, side, caps, q_len,
):
    groups = lax.axis_size("grp")
    shards = 2 * side * side
    chips = side * side
    tok_rows, width = states.shape
    part = w_gate.shape[0]
    dim = w_proj.shape[1]
    passages, toks = cent_ids.shape
    dims, count = table.shape
    chunks = 8
    block = width // shards
    tokens = groups * tok_rows
    spread = jnp.broadcast_to(bucket[:, :, None], (4, dims, toks))
    vmem = pl.BlockSpec(memory_space=pltpu.VMEM)
    smem = pl.BlockSpec(memory_space=pltpu.SMEM)
    bf16, f32 = jnp.bfloat16, jnp.float32
    dma = pltpu.SemaphoreType.DMA
    wide = (chips, 3, block, part)
    return pl.pallas_call(
        functools.partial(step_kernel, side, groups, chunks),
        out_shape=(jax.ShapeDtypeStruct((8, 128), f32),)
        + (jax.ShapeDtypeStruct((block, part), f32),) * 3
        + (jax.ShapeDtypeStruct((block // groups, dim), f32),),
        in_specs=[vmem] * 7 + [smem] * 2 + [vmem] * 5 + [pl.BlockSpec(memory_space=pl.ANY)],
        out_specs=(vmem,) * 5,
        scratch_shapes=[
            pltpu.VMEM((dims, count), bf16),
            pltpu.VMEM((groups, passages, dims, toks), bf16),
            pltpu.VMEM((groups, tok_rows, width), bf16),
            pltpu.VMEM((groups, tok_rows, part), bf16),
            pltpu.VMEM((groups, tok_rows, part), bf16),
            pltpu.VMEM((groups, tok_rows, part), bf16),
            pltpu.VMEM((groups, tok_rows, width), bf16),
            pltpu.VMEM((tok_rows, width), f32),
            pltpu.VMEM((groups - 1, tok_rows, width), bf16),
            pltpu.VMEM((tok_rows, width), f32),
            pltpu.VMEM((width, tok_rows), bf16),
            pltpu.VMEM((tok_rows, dim), f32),
            pltpu.VMEM((shards, 1, 128), jnp.int32),
            pltpu.SMEM((shards, 1, 128), jnp.int32),
            pltpu.VMEM((shards, tok_rows // q_len, q_len, dim), bf16),
            pltpu.VMEM((shards, caps, q_len, dim), bf16),
            pltpu.VMEM((shards, 8, dim), f32),
            pltpu.VMEM((shards, caps, q_len, dim), bf16),
            pltpu.VMEM((shards, 8, dim), f32),
            pltpu.VMEM((tok_rows // q_len, shards, 8, dim), f32),
            pltpu.VMEM((groups, tok_rows, width), bf16),
            pltpu.VMEM((chips, 2, block, tokens), bf16),
            pltpu.VMEM((chips, 2, block, tokens), bf16),
            pltpu.VMEM((groups, tok_rows, part), bf16),
            pltpu.VMEM((groups, tok_rows, part), bf16),
            pltpu.VMEM(wide, bf16),
            pltpu.VMEM(wide, bf16),
            pltpu.VMEM(wide, bf16),
            pltpu.VMEM((chips - 1, 3, block, part), bf16),
            pltpu.VMEM((chips, 2, block, dim), f32),
            pltpu.VMEM((chips, block, dim), f32),
            pltpu.VMEM((chips, block, dim), f32),
            pltpu.VMEM((chips - 1, block, dim), f32),
            pltpu.VMEM((groups, block // groups, dim), f32),
            pltpu.VMEM((groups - 1, block // groups, dim), f32),
            dma((8,)),
            dma,
        ]
        + [dma((groups,))] * 8
        + [dma((chunks, groups))] * 2
        + [dma((shards,))] * 8
        + [dma((side + 1,))] * 2
        + [dma((2, chips - 1))] * 2,
        compiler_params=pltpu.CompilerParams(
            collective_id=0, has_side_effects=True, vmem_limit_bytes=60 << 20
        ),
        cost_estimate=pl.CostEstimate(flops=0, bytes_accessed=300_000_000, transcendentals=0),
    )(
        states, norm_gain, final_gain, w_gate, w_up, w_down_t, w_proj, cent_ids >> 7, lens,
        cent_ids & 127, codes, spread, tables, which, table,
    )


def coords(shape):
    me = lax.axis_index("shard")
    return me // (2 * shape), (me // 2) % shape, me % 2, lax.axis_index("grp")


def ranks(hits):
    count = hits.shape[1]
    before = lax.broadcasted_iota(jnp.int32, (count, count), 0) < lax.broadcasted_iota(
        jnp.int32, (count, count), 1
    )
    return jnp.dot(
        hits.astype(jnp.bfloat16), before.astype(jnp.bfloat16), preferred_element_type=jnp.float32
    ).astype(jnp.int32)


def slots(hits, caps):
    nth = lax.broadcasted_iota(jnp.int32, (1, caps, 1), 1)
    return hits[:, None, :] & (ranks(hits)[:, None, :] == nth)


def local(
    query_states,
    norm_gain,
    final_gain,
    w_gate,
    w_up,
    w_down_t,
    w_proj,
    centroids,
    bucket_values,
    centroid_ids,
    residual_codes,
    passage_lens,
    negative_ids,
):
    q_dev, q_len, width = query_states.shape
    dim = w_proj.shape[1]
    shards = lax.axis_size("shard")
    side = math.isqrt(shards // 2)
    cands = negative_ids.shape[1]
    tok_rows = q_dev * q_len
    local_pass = centroid_ids.shape[0]
    caps = 2 * q_dev * cands // shards
    me = lax.axis_index("shard")

    flat_ids = negative_ids.reshape(1, -1)
    owner = lax.broadcasted_iota(jnp.int32, (shards, 1), 0)
    places = lax.broadcasted_iota(jnp.int32, (1, 1, q_dev * cands), 2)
    sent = slots(flat_ids // local_pass == owner, caps)
    place = jnp.sum(jnp.where(sent, places, 0), axis=2)
    asked = jnp.sum(jnp.where(sent, (flat_ids % local_pass)[:, None, :], 0), axis=2)
    tables = jnp.concatenate(
        [asked, place // cands, jnp.zeros((shards, 128 - 2 * caps), jnp.int32)], axis=1
    ).reshape(shards, 1, 128)
    lens = lax.dynamic_slice(passage_lens, (me * local_pass,), (local_pass,))
    states = query_states.reshape(tok_rows, width)
    filled = jnp.any(sent, axis=2)[:, :, None]
    query = lax.broadcasted_iota(jnp.int32, (1, 1, 128), 2)
    mine = filled & ((place // cands)[:, :, None] == query)
    first = mine & ((place % cands)[:, :, None] == 0)
    which = mine.astype(jnp.int32) + first.astype(jnp.int32)
    which = jnp.pad(which, ((0, 0), (0, 8 - caps), (0, 0))).reshape(shards * 8, 128)
    losses, grad_gate, grad_up, grad_down, grad_proj = step_call(
        states, norm_gain.reshape(1, -1), final_gain.reshape(1, -1), w_gate.T, w_up.T, w_down_t.T,
        w_proj, centroid_ids, lens, residual_codes, bucket_values, tables, which, centroids, side,
        caps, q_len,
    )
    return (losses[0, :q_dev], grad_gate, grad_up, grad_down, grad_proj)


def solution(mesh):
    placed = (
        P(("shard", "grp"), None, None),
        P(),
        P(),
        P(None, "grp"),
        P(None, "grp"),
        P(None, "grp"),
        P(),
        P("grp", None),
        P(None, "grp"),
        P("shard", None),
        P("shard", "grp", None),
        P(),
        P(("shard", "grp"), None),
    )
    return jax.shard_map(
        local,
        mesh=mesh,
        in_specs=placed,
        out_specs=(
            P(("shard", "grp")),
            P("shard", "grp"),
            P("shard", "grp"),
            P("shard", "grp"),
            P(("shard", "grp"), None),
        ),
        check_vma=False,
    )
```

time: 238 us -> 187 us (0.79)
  waiting for transfers between devices: 16.2 us -> 0 us
  matrix products: 14.5 us -> 0.13 us
  Pallas kernels: 156 us -> 170 us
  between operations: 14.3 us -> 0.69 us
  local copies, waits for them, and re-layouts: 24.4 us -> 11.5 us
  other arithmetic: 8.64 us -> 2.77 us
    all_gather x1 -> x0, waiting for transfers between devices: 16.2 us -> none  [local(): group_grad = lax.all_gather(dout_b, 'grp', axis=0, tiled=True)]
    dot_general x7 -> x0, matrix products: 14.4 us -> none  [the longest x1 3.97 us: local(): lax.dot_general(group_rows, dgate, contract, preferred_element_type=jnp.f...]
    pallas_call x2 -> x1, Pallas kernels: 156 us -> 170 us  [step_call(): pl.pallas_call(functools.partial(step_kernel, side, groups, chunks), out_...]
    convert_element_type x6 -> x0, local copies, waits for them, and re-layouts: 9.1 us -> none  [the longest x1 2.56 us: local(): term_gate.astype(jnp.bfloat16)]
    unnamed x37 -> x4, local copies, waits for them, and re-layouts: 11.8 us -> 5.88 us
    convert_element_type x5 -> x0, other arithmetic: 2.62 us -> none  [the longest x1 1.6 us: local(): dup = (dhid * gelu.astype(jnp.float32)).astype(jnp.bfloat16)]
  transfers between devices with their start and end apart: 1 -> 0, of which waited for: 1 -> 0; matrix products, arithmetic and copies ran while one was open for 3% -> 0% of each run, Pallas kernels for 0% -> 0%
where the time goes in v3:
time: 187 us; the launch traced here: 185 us
  Pallas kernels  170 us (91%)
  local copies, waits for them, and re-layouts  11.5 us (6%)
  other arithmetic  2.77 us (1%)
    pallas_call x1, Pallas kernels, step_call(): pl.pallas_call(functools.partial(step_kernel, side, groups, chunks), out_...  170 us
    unnamed x4, local copies, waits for them, and re-layouts  5.88 us

profile of v3, /device:TPU:0, one launch (start us, length us, event | category | flops | bytes accessed | tf_op | source)
XLA Modules:
  0.0 185.0 jit_solution(11544022756380355939)
XLA Ops:
  0.6 1.3 dynamic_slice.3.lens_ref
  1.9 0.8 reshape.171
  2.7 0.1 pad.7.clone
  2.8 0.1 convolution_convert_fusion
  2.9 0.1 fusion.1
  3.1 0.2 select_reduce_fusion.1
  3.3 0.1 copy.23
  3.4 0.1 copy.22
  3.5 0.1 copy.18
  3.6 0.7 add_add_fusion
  4.3 0.2 convert_add_fusion
  4.5 0.6 pad_bitcast_fusion.which_ref
  5.1 1.4 broadcast_in_dim.33.bucket_ref
  6.5 1.5 broadcast_and_fusion
  8.0 169.9 %shard_map.164 = (f32[8,128]{1,0:T(8,128)}, f32[32,656]{1,0:T(8,128)}, f32[32,656]{1,0:T(8,128)}, f32[32,656]{1,0:T(8,128)}, f32[8,128]{1,0:T(8,128)}) custom-call(bf16[128,1024]{1,0:T(8,128)(2,1)} %bitcast.14, f32[1,1024]{1,0:T(1,128)} %bitcast.16, f32[1,1024]{1,0:T(1,128)} %bitcast.17, bf16[656,1024]{1,0:T(8,128)(2,1)} %bitcast.11, ...), custom_call_target="tpu_custom_call" | custom-call | bytes 300000000 | tf_op jit(solution)/shard_map/pallas_call | solution.py:547
  177.9 1.2 slice_bitcast_fusion
  179.1 1.5 copy.28
  180.6 1.5 copy.29
  182.2 1.5 copy.30
  183.7 1.3 copy.31
  (5 shorter events, 0.1 us)

commit v4 on v3

--- a/solution.py
+++ b/solution.py
@@ -69,13 +69,14 @@
     states_ref, norm_gain_ref, final_gain_ref, gate_w, up_w, down_w, proj_w,
     blk_ref, lens_ref, lane_ref, codes_ref, bucket_ref, tables_ref, which_ref, tab_hbm,
     loss_ref, gate_out, up_out, down_out, proj_out,
-    tab, docs, rows_ref, slope_ref, gelu_ref, hidden_ref, part, part_own, part_land, out_ref,
+    tab, docs, rows_ref, slope_ref, gelu_ref, hidden_ref, part, part_own, part_tmp, part_in, out_ref,
     final_t, proj_ref, asks, asks_smem, queries, pull_out, score_out, pull_ref, score_ref,
-    weights, douts, rows_t, douts_t, dgate, dup, first, twin, held, land,
+    weights, douts, rows_t, douts_t, dgate, dup, first, twin, held,
+    tmp_one, in_one, mids, tmp_two, in_two,
     proj_term, twin_proj, held_proj, land_proj, rows_sum, land_grp,
-    tab_sem, asks_sem, rows_send, rows_recv, part_send, part_recv, dout_send, dout_recv,
-    grp_send, grp_recv, docs_send, docs_recv,
-    asks_send, asks_recv, query_send, query_recv, pull_send, pull_recv, score_send, score_recv,
+    tab_sem, asks_sem, rows_send, rows_recv, dout_send, dout_recv,
+    grp_send, grp_recv, docs_send, docs_recv, ring_send, ring_recv,
+    asks_send, asks_recv, pull_send, pull_recv, score_send, score_recv,
     twin_send, twin_recv, chip_send, chip_recv,
 ):
     z, x, core, grp = coords(side)
@@ -129,25 +130,94 @@
             device_id=(me, (grp + step) % groups), device_id_type=MESH,
         )
 
-    def came(step):
-        return (grp + groups - step) % groups
-
-    def rows_copy(step, slot):
-        return along_grp(
-            step, rows_ref.at[slot], rows_ref.at[slot], rows_send.at[step], rows_recv.at[step]
-        )
-
-    def part_copy(step):
-        return along_grp(
-            step, part.at[(grp + step) % groups], part_land.at[step - 1],
-            part_send.at[step], part_recv.at[step],
-        )
-
-    def docs_copy(step, chunk, slot):
-        place = docs.at[slot, pl.ds(chunk * span, span)]
-        return along_grp(
-            step, place, place, docs_send.at[chunk, step], docs_recv.at[chunk, step]
-        )
+    left, right, across = (grp + groups - 1) % groups, (grp + 1) % groups, (grp + 2) % groups
+
+    def spread_grp(view, send_sem, recv_sem):
+        def copy(j, incoming):
+            slot = ((left, right, across, across) if incoming else (grp, grp, left, right))[j]
+            place = view(slot, None if j < 2 else j - 2)
+            return pltpu.make_async_remote_copy(
+                src_ref=place, dst_ref=place, send_sem=send_sem(j), recv_sem=recv_sem(j),
+                device_id=(me, left if j % 2 else right), device_id_type=MESH,
+            )
+
+        return copy
+
+    def rows_view(ref):
+        half = tok_rows // 2
+        return lambda slot, part: (
+            ref.at[slot] if part is None else ref.at[slot, pl.ds(part * half, half)]
+        )
+
+    rows_copy = spread_grp(
+        rows_view(rows_ref), lambda j: rows_send.at[j], lambda j: rows_recv.at[j]
+    )
+    dout_copy = spread_grp(rows_view(douts), lambda j: dout_send.at[j], lambda j: dout_recv.at[j])
+
+    def docs_copies(c):
+        half = span // 2
+        return spread_grp(
+            lambda slot, part: (
+                docs.at[slot, pl.ds(c * span, span)]
+                if part is None
+                else docs.at[slot, pl.ds(c * span + part * half, half)]
+            ),
+            lambda j: docs_send.at[c, j],
+            lambda j: docs_recv.at[c, j],
+        )
+
+    def docs_own(c):
+        copy = docs_copies(c)
+        copy(0, False).start()
+        copy(1, False).start()
+
+    def docs_forward(c):
+        copy = docs_copies(c)
+        for j in range(2):
+            copy(j, True).wait_recv()
+            copy(j + 2, False).start()
+
+    def sum_ring(n, lower, upper, view, tmp, into):
+        def copy(j):
+            src = (view(2, 0), view(2, 1), view(3, None), view(1, None))[j]
+            return pltpu.make_async_remote_copy(
+                src_ref=src, dst_ref=(tmp.at[j] if j < 2 else into.at[j - 2]),
+                send_sem=ring_send.at[n, j], recv_sem=ring_recv.at[n, j],
+                device_id=upper if j % 2 else lower, device_id_type=MESH,
+            )
+
+        def start():
+            copy(0).start()
+            copy(1).start()
+
+        def middle():
+            for j in range(2):
+                copy(j).wait_recv()
+                place = view(1 if j else 3, j)
+                place[...] = (
+                    place[...].astype(jnp.float32) + tmp[j].astype(jnp.float32)
+                ).astype(jnp.bfloat16)
+                copy(j + 2).start()
+
+        def end():
+            copy(2).wait_recv()
+            copy(3).wait_recv()
+            return into[0].astype(jnp.float32) + into[1].astype(jnp.float32)
+
+        def sent():
+            for j in range(4):
+                copy(j).wait_send()
+
+        return start, middle, end, sent
+
+    def part_view(k, half):
+        slot = (grp + k) % groups
+        rows = tok_rows // 2
+        return part.at[slot] if half is None else part.at[slot, pl.ds(half * rows, rows)]
+
+    part_start, part_middle, part_end, part_sent = sum_ring(
+        0, (me, left), (me, right), part_view, part_tmp, part_in
+    )
 
     def along_shard(step, src, dst, send_sems, recv_sems):
         return pltpu.make_async_remote_copy(
@@ -158,8 +228,30 @@
     def asks_copy(step, slot):
         return along_shard(step, tables_ref.at[to(step)], asks.at[slot], asks_send, asks_recv)
 
+    chips = side * side
+    chip = me // 2
+
+    def chip_to(step):
+        return ((z + step // side) % side) * side + (x + step % side) % side
+
+    def chip_from(step):
+        return ((z + side - step // side) % side) * side + (x + side - step % side) % side
+
     def query_copy(step, slot):
-        return along_shard(step, queries.at[me], queries.at[slot], query_send, query_recv)
+        return pltpu.make_async_remote_copy(
+            src_ref=queries.at[chip, core], dst_ref=queries.at[slot, core],
+            send_sem=chip_send.at[1, step - 1], recv_sem=chip_recv.at[1, step - 1],
+            device_id=(chip_to(step) * 2 + core, grp), device_id_type=MESH,
+        )
+
+    def swap(src, dst, i):
+        return pltpu.make_async_remote_copy(
+            src_ref=src, dst_ref=dst, send_sem=twin_send.at[i], recv_sem=twin_recv.at[i],
+            device_id=(chip * 2 + 1 - core, grp), device_id_type=MESH,
+        )
+
+    def query_swap(of):
+        return swap(queries.at[:, of], queries.at[:, of], side + 1)
 
     def back(step, src, dst, send_sems, recv_sems):
         return pltpu.make_async_remote_copy(
@@ -173,8 +265,8 @@
     def score_copy(step, slot):
         return back(step, score_out.at[source(step)], score_ref.at[slot], score_send, score_recv)
 
-    for step in range(1, groups):
-        rows_copy(step, grp).start()
+    rows_copy(0, False).start()
+    rows_copy(1, False).start()
 
     def ask(step, carry):
         asks_copy(step, me).start()
@@ -182,12 +274,15 @@
 
     lax.fori_loop(1, shards, ask, 0)
     asks[me] = tables_ref[me]
+    for j in range(2):
+        rows_copy(j, True).wait_recv()
+        rows_copy(j + 2, False).start()
     for copy in table_copies:
         copy.wait()
 
     def feed_forward():
-        for step in range(1, groups):
-            rows_copy(step, came(step)).wait_recv()
+        rows_copy(2, True).wait_recv()
+        rows_copy(3, True).wait_recv()
 
         def block(r, carry):
             normed = rows_ref[r]
@@ -210,27 +305,23 @@
             return carry
 
         lax.fori_loop(0, groups, block, 0)
-        for step in range(1, groups):
-            part_copy(step).start()
+        part_start()
 
     def make_queries():
-        out = states_ref[...].astype(jnp.float32) + part_own[...]
-        for step in range(1, groups):
-            part_copy(step).wait_recv()
-            out = out + part_land[step - 1].astype(jnp.float32)
+        out = states_ref[...].astype(jnp.float32) + part_own[...] + part_end()
         out_ref[...] = out
         final = layer_norm(out, final_gain_ref[...]).astype(jnp.bfloat16)
         final_t[...] = final.T
         proj = jnp.dot(final, proj_w[...], preferred_element_type=jnp.float32)
         proj_ref[...] = proj
         scale = lax.rsqrt(jnp.mean(proj * proj, axis=-1, keepdims=True) + 1e-06) / math.sqrt(dim)
-        queries[me] = (proj * scale).astype(jnp.bfloat16).reshape(tok_rows // q_len, q_len, dim)
+        queries[chip, core] = (proj * scale).astype(jnp.bfloat16).reshape(tok_rows // q_len, q_len, dim)
 
         def tell(step, carry):
-            query_copy(step, me).start()
+            query_copy(step, chip).start()
             return carry
 
-        lax.fori_loop(1, shards, tell, 0)
+        lax.fori_loop(1, chips, tell, 0)
 
     def chunk_of(c, carry):
         def passage(i, carry):
@@ -239,17 +330,26 @@
             return carry
 
         lax.fori_loop(0, span, passage, 0)
-        for step in range(1, groups):
-            docs_copy(step, c, grp).start()
+        docs_own(c)
+        pl.when(c > 0)(lambda: docs_forward(c - 1))
         pl.when(c == 0)(feed_forward)
-        pl.when(c == chunks // 2)(make_queries)
+        pl.when(c == 1)(part_middle)
+        pl.when(c == 3)(make_queries)
         return carry
 
     lax.fori_loop(0, chunks, chunk_of, 0)
+
+    docs_forward(chunks - 1)
+
+    def queries_in(step, carry):
+        query_copy(step, chip_from(step)).wait_recv()
+        return carry
+
+    lax.fori_loop(1, chips, queries_in, 0)
+    query_swap(core).start()
 
     def gather_in(step, carry):
         asks_copy(step, source(step)).wait_recv()
-        query_copy(step, source(step)).wait_recv()
         return carry
 
     lax.fori_loop(1, shards, gather_in, 0)
@@ -257,9 +357,11 @@
     to_smem.start()
     to_smem.wait()
 
+    query_swap(1 - core).wait_recv()
+
     def docs_in(c, carry):
-        for step in range(1, groups):
-            docs_copy(step, c, came(step)).wait_recv()
+        docs_copies(c)(2, True).wait_recv()
+        docs_copies(c)(3, True).wait_recv()
         return carry
 
     lax.fori_loop(0, chunks, docs_in, 0)
@@ -270,7 +372,7 @@
         for k in range(caps):
             p = asks_smem[d, 0, k]
             raw = jnp.concatenate([docs[g, p] for g in range(groups)], axis=0)
-            pull, score = pair(raw, queries[d, asks_smem[d, 0, caps + k]], lens_ref[p])
+            pull, score = pair(raw, queries[d // 2, d % 2, asks_smem[d, 0, caps + k]], lens_ref[p])
             pull_out[d, k] = pull
             rows.append(jnp.broadcast_to(score, (1, dim)))
         score_out[d] = jnp.concatenate(rows + [jnp.zeros((8 - caps, dim), jnp.float32)], axis=0)
@@ -344,31 +446,15 @@
     )
     douts[grp] = dout.astype(jnp.bfloat16)
 
-    def dout_copy(step, slot):
-        return along_grp(
-            step, douts.at[slot], douts.at[slot], dout_send.at[step], dout_recv.at[step]
-        )
-
-    for step in range(1, groups):
-        dout_copy(step, grp).start()
-
-    chips = side * side
-    chip = me // 2
+    dout_copy(0, False).start()
+    dout_copy(1, False).start()
+
     block = rows_t.shape[2]
 
-    def swap(src, dst, i):
+    def chip_copy(step):
         return pltpu.make_async_remote_copy(
-            src_ref=src, dst_ref=dst, send_sem=twin_send.at[i], recv_sem=twin_recv.at[i],
-            device_id=(chip * 2 + 1 - core, grp), device_id_type=MESH,
-        )
-
-    def chip_to(step):
-        return ((z + step // side) % side) * side + (x + step % side) % side
-
-    def chip_copy(step, src, dst, kind):
-        return pltpu.make_async_remote_copy(
-            src_ref=src.at[chip_to(step)], dst_ref=dst.at[step - 1],
-            send_sem=chip_send.at[kind, step - 1], recv_sem=chip_recv.at[kind, step - 1],
+            src_ref=held_proj.at[chip_to(step)], dst_ref=land_proj.at[step - 1],
+            send_sem=chip_send.at[0, step - 1], recv_sem=chip_recv.at[0, step - 1],
             device_id=(chip_to(step) * 2 + core, grp), device_id_type=MESH,
         )
 
@@ -379,11 +465,18 @@
     proj_swap.start()
 
     def spread_back(i, carry):
-        @pl.when(i > 0)
+        @pl.when(i == 1)
         def _():
-            dout_copy(i, (grp + groups - i) % groups).wait_recv()
-
-        r = (grp + groups - i) % groups
+            for j in range(2):
+                dout_copy(j, True).wait_recv()
+                dout_copy(j + 2, False).start()
+
+        @pl.when(i == 3)
+        def _():
+            dout_copy(2, True).wait_recv()
+            dout_copy(3, True).wait_recv()
+
+        r = (grp + i + i // 2 - 2 * (i // 3)) % groups
         dhid = dot_t(douts[r], down_w[...])
         dgate[r] = (dhid * slope_ref[r].astype(jnp.float32)).astype(jnp.bfloat16)
         dup[r] = (dhid * gelu_ref[r].astype(jnp.float32)).astype(jnp.bfloat16)
@@ -403,55 +496,87 @@
     lax.fori_loop(0, chips, add_proj, 0)
 
     def send_proj(step, carry):
-        chip_copy(step, held_proj, land_proj, 0).start()
+        chip_copy(step).start()
         return carry
 
     lax.fori_loop(1, chips, send_proj, 0)
 
     tokens = groups * tok_rows
 
-    def term(i, start, half):
-        left = (rows_t, rows_t, douts_t)[i]
-        right = (dgate, dup, hidden_ref)[i]
-        return jnp.dot(
-            left[pl.ds(start, side), half].reshape(side * block, tokens),
-            right[...].reshape(tokens, right.shape[2]),
-            preferred_element_type=jnp.float32,
-        ).reshape(side, block, right.shape[2])
-
-    def band(i):
-        return ((z + 1 + i) % side) * side
+    main = gate_out.shape[1] // 128 * 128
+    rest = gate_out.shape[1] - main
+
+    def terms(row, half):
+        found = []
+        for lhs, rhs in ((rows_t, dgate), (rows_t, dup), (douts_t, hidden_ref)):
+            found.append(
+                jnp.dot(
+                    lhs[pl.ds(row * side, side), half].reshape(side * block, tokens),
+                    rhs[...].reshape(tokens, main + rest),
+                    preferred_element_type=jnp.float32,
+                )
+            )
+        fill = jnp.zeros((side * block, held.shape[3] - 3 * (main + rest)), jnp.float32)
+        return jnp.concatenate(
+            [t[:, :main] for t in found] + [t[:, main:] for t in found] + [fill], axis=1
+        ).reshape(side, block, held.shape[3])
+
+    def row_of(i):
+        return (z + 2 + i) % side
 
     def swap_copy(i):
-        return swap(first.at[pl.ds(band(i), side)], twin.at[pl.ds(band(i), side)], i)
+        return swap(first.at[row_of(i)], twin.at[row_of(i)], i)
 
     def give(i, carry):
-        for n in range(3):
-            first[pl.ds(band(i), side), n] = term(n, band(i), 1 - core).astype(jnp.bfloat16)
+        first[row_of(i)] = terms(row_of(i), 1 - core).astype(jnp.bfloat16)
         swap_copy(i).start()
         return carry
 
     lax.fori_loop(0, side, give, 0)
+
+    cols = held.shape[3] // 2
+    few = side // 2
+    x_low = ((z * side + (x + side - 1) % side) * 2 + core, grp)
+    x_high = ((z * side + (x + 1) % side) * 2 + core, grp)
+    z_low = ((((z + side - 1) % side) * side + x) * 2 + core, grp)
+    z_high = ((((z + 1) % side) * side + x) * 2 + core, grp)
+
+    def view_x(k, half):
+        rows = pl.ds(0, side) if half is None else pl.ds(half * few, few)
+        return held.at[rows, (x + k) % side, :, pl.ds(0, cols)]
+
+    def view_z(k, half):
+        rows = pl.ds(0, side) if half is None else pl.ds(half * few, few)
+        return held.at[(z + k) % side, rows, :, pl.ds(cols, cols)]
+
+    def view_mid(n, place):
+        def view(k, half):
+            spot = (place + k) % side
+            part = block // 2
+            return mids.at[n, spot] if half is None else mids.at[n, spot, pl.ds(half * part, part)]
+
+        return view
+
+    ring_x = sum_ring(1, x_low, x_high, view_x, tmp_one.at[0], in_one.at[0])
+    ring_z = sum_ring(2, z_low, z_high, view_z, tmp_one.at[1], in_one.at[1])
+    then_z = sum_ring(3, z_low, z_high, view_mid(0, z), tmp_two.at[0], in_two.at[0])
+    then_x = sum_ring(4, x_low, x_high, view_mid(1, x), tmp_two.at[1], in_two.at[1])
 
     def keep(i, carry):
         swap_copy(i).wait_recv()
-        for n in range(3):
-            held[pl.ds(band(i), side), n] = (
-                term(n, band(i), core) + twin[pl.ds(band(i), side), n].astype(jnp.float32)
-            ).astype(jnp.bfloat16)
-        for dx in range(side):
-            step = ((1 + i) % side) * side + dx
-
-            @pl.when(step > 0)
-            def _():
-                chip_copy(step, held, land, 1).start()
-
+        held[row_of(i)] = (
+            terms(row_of(i), core) + twin[row_of(i)].astype(jnp.float32)
+        ).astype(jnp.bfloat16)
+        pl.when(i == 0)(ring_z[0])
         return carry
 
     lax.fori_loop(0, side, keep, 0)
+    ring_x[0]()
+    ring_z[1]()
+    ring_x[1]()
 
     def proj_in(step, total):
-        chip_copy(step, held_proj, land_proj, 0).wait_recv()
+        chip_copy(step).wait_recv()
         return total + land_proj[step - 1]
 
     rows_sum[...] = lax.fori_loop(1, chips, proj_in, held_proj[chip]).reshape(rows_sum.shape)
@@ -470,40 +595,43 @@
         mine = mine + land_grp[step - 1]
     proj_out[...] = mine
 
+    mids[1] = (view_z(0, None)[...].astype(jnp.float32) + ring_z[2]()).astype(jnp.bfloat16)
+    then_x[0]()
+    mids[0] = (view_x(0, None)[...].astype(jnp.float32) + ring_x[2]()).astype(jnp.bfloat16)
+    then_z[0]()
+    then_x[1]()
+    then_z[1]()
+    whole = jnp.concatenate(
+        [
+            mids[0, z].astype(jnp.float32) + then_z[2](),
+            mids[1, x].astype(jnp.float32) + then_x[2](),
+        ],
+        axis=1,
+    )
     for n, ref in enumerate((gate_out, up_out, down_out)):
-        ref[...] = held[chip, n].astype(jnp.float32)
-
-    def sum_in(i, carry):
-        for dx in range(side):
-            step = ((1 + i) % side) * side + dx
-
-            @pl.when(step > 0)
-            def _():
-                chip_copy(step, held, land, 1).wait_recv()
-                for n, ref in enumerate((gate_out, up_out, down_out)):
-                    ref[...] += land[step - 1, n].astype(jnp.float32)
-
-        return carry
-
-    lax.fori_loop(0, side, sum_in, 0)
+        ref[:, :main] = whole[:, n * main : (n + 1) * main]
+        ref[:, main:] = whole[:, 3 * main + n * rest : 3 * main + (n + 1) * rest]
 
     def sent(step, carry):
         asks_copy(step, me).wait_send()
-        query_copy(step, me).wait_send()
         pull_copy(step, me).wait_send()
         score_copy(step, me).wait_send()
         return carry
 
     lax.fori_loop(1, shards, sent, 0)
     for step in range(1, groups):
-        rows_copy(step, grp).wait_send()
-        part_copy(step).wait_send()
-        dout_copy(step, grp).wait_send()
         sum_copy(step).wait_send()
+    for j in range(4):
+        rows_copy(j, False).wait_send()
+        dout_copy(j, False).wait_send()
+    for ring in (ring_x, ring_z, then_x, then_z):
+        ring[3]()
+    part_sent()
+    query_swap(core).wait_send()
 
     def docs_out(c, carry):
-        for step in range(1, groups):
-            docs_copy(step, c, grp).wait_send()
+        for j in range(4):
+            docs_copies(c)(j, False).wait_send()
         return carry
 
     lax.fori_loop(0, chunks, docs_out, 0)
@@ -516,8 +644,8 @@
     lax.fori_loop(0, side, swapped, 0)
 
     def chips_out(step, carry):
-        chip_copy(step, held_proj, land_proj, 0).wait_send()
-        chip_copy(step, held, land, 1).wait_send()
+        chip_copy(step).wait_send()
+        query_copy(step, chip).wait_send()
         return carry
 
     lax.fori_loop(1, chips, chips_out, 0)
@@ -543,7 +671,8 @@
     smem = pl.BlockSpec(memory_space=pltpu.SMEM)
     bf16, f32 = jnp.bfloat16, jnp.float32
     dma = pltpu.SemaphoreType.DMA
-    wide = (chips, 3, block, part)
+    wide = (side, side, block, -(-3 * part // 256) * 256)
+    cols = wide[3] // 2
     return pl.pallas_call(
         functools.partial(step_kernel, side, groups, chunks),
         out_shape=(jax.ShapeDtypeStruct((8, 128), f32),)
@@ -560,13 +689,14 @@
             pltpu.VMEM((groups, tok_rows, part), bf16),
             pltpu.VMEM((groups, tok_rows, width), bf16),
             pltpu.VMEM((tok_rows, width), f32),
-            pltpu.VMEM((groups - 1, tok_rows, width), bf16),
+            pltpu.VMEM((2, tok_rows // 2, width), bf16),
+            pltpu.VMEM((2, tok_rows, width), bf16),
             pltpu.VMEM((tok_rows, width), f32),
             pltpu.VMEM((width, tok_rows), bf16),
             pltpu.VMEM((tok_rows, dim), f32),
             pltpu.VMEM((shards, 1, 128), jnp.int32),
             pltpu.SMEM((shards, 1, 128), jnp.int32),
-            pltpu.VMEM((shards, tok_rows // q_len, q_len, dim), bf16),
+            pltpu.VMEM((chips, 2, tok_rows // q_len, q_len, dim), bf16),
             pltpu.VMEM((shards, caps, q_len, dim), bf16),
             pltpu.VMEM((shards, 8, dim), f32),
             pltpu.VMEM((shards, caps, q_len, dim), bf16),
@@ -580,7 +710,11 @@
             pltpu.VMEM(wide, bf16),
             pltpu.VMEM(wide, bf16),
             pltpu.VMEM(wide, bf16),
-            pltpu.VMEM((chips - 1, 3, block, part), bf16),
+            pltpu.VMEM((2, 2, side // 2, block, cols), bf16),
+            pltpu.VMEM((2, 2, side, block, cols), bf16),
+            pltpu.VMEM((2, side, block, cols), bf16),
+            pltpu.VMEM((2, 2, block // 2, cols), bf16),
+            pltpu.VMEM((2, 2, block, cols), bf16),
             pltpu.VMEM((chips, 2, block, dim), f32),
             pltpu.VMEM((chips, block, dim), f32),
             pltpu.VMEM((chips, block, dim), f32),
@@ -590,10 +724,11 @@
             dma((8,)),
             dma,
         ]
-        + [dma((groups,))] * 8
+        + [dma((groups,))] * 6
         + [dma((chunks, groups))] * 2
-        + [dma((shards,))] * 8
-        + [dma((side + 1,))] * 2
+        + [dma((5, groups))] * 2
+        + [dma((shards,))] * 6
+        + [dma((side + 2,))] * 2
         + [dma((2, chips - 1))] * 2,
         compiler_params=pltpu.CompilerParams(
             collective_id=0, has_side_effects=True, vmem_limit_bytes=60 << 20

time: 187 us -> 170 us (0.909)
  Pallas kernels: 170 us -> 154 us
    pallas_call x1, Pallas kernels: 170 us -> 154 us  [step_call(): pl.pallas_call(functools.partial(step_kernel, side, groups, chunks), out_...]
where the time goes in v4:
time: 170 us; the launch traced here: 169 us
  Pallas kernels  154 us (91%)
  local copies, waits for them, and re-layouts  11.5 us (7%)
  other arithmetic  2.77 us (2%)
    pallas_call x1, Pallas kernels, step_call(): pl.pallas_call(functools.partial(step_kernel, side, groups, chunks), out_...  154 us
    unnamed x4, local copies, waits for them, and re-layouts  5.88 us

profile of v4, /device:TPU:0, one launch (start us, length us, event | category | flops | bytes accessed | tf_op | source)
XLA Modules:
  0.0 169.4 jit_solution(9610798257318173592)
XLA Ops:
  0.6 1.3 dynamic_slice.3.lens_ref
  1.9 0.8 reshape.171
  2.7 0.1 pad.7.clone
  2.8 0.1 convolution_convert_fusion
  2.9 0.1 fusion.1
  3.1 0.2 select_reduce_fusion.1
  3.3 0.1 copy.23
  3.4 0.1 copy.22
  3.5 0.1 copy.18
  3.6 0.7 add_add_fusion
  4.3 0.2 convert_add_fusion
  4.5 0.6 pad_bitcast_fusion.which_ref
  5.1 1.4 broadcast_in_dim.33.bucket_ref
  6.5 1.5 broadcast_and_fusion
  8.0 154.3 %shard_map.164 = (f32[8,128]{1,0:T(8,128)}, f32[32,656]{1,0:T(8,128)}, f32[32,656]{1,0:T(8,128)}, f32[32,656]{1,0:T(8,128)}, f32[8,128]{1,0:T(8,128)}) custom-call(bf16[128,1024]{1,0:T(8,128)(2,1)} %bitcast.14, f32[1,1024]{1,0:T(1,128)} %bitcast.16, f32[1,1024]{1,0:T(1,128)} %bitcast.17, bf16[656,1024]{1,0:T(8,128)(2,1)} %bitcast.11, ...), custom_call_target="tpu_custom_call" | custom-call | bytes 300000000 | tf_op jit(solution)/shard_map/pallas_call | solution.py:676
  162.3 1.2 slice_bitcast_fusion
  163.5 1.5 copy.28
  165.1 1.5 copy.29
  166.6 1.5 copy.30
  168.2 1.3 copy.31
  (5 shorter events, 0.1 us)

commit v5 on v4

--- a/solution.py
+++ b/solution.py
@@ -25,7 +25,8 @@
     base = jnp.zeros((dims, toks), jnp.float32)
     for j in range(toks):
         block = tab[:, pl.ds(blk_ref[p, j] * 128, 128)].astype(jnp.float32)
-        base = jnp.where(lane == j, jnp.take_along_axis(block, spot, axis=1), base)
+        near = jnp.take_along_axis(block, spot, axis=1, mode="promise_in_bounds")
+        base = jnp.where(lane == j, near, base)
     words = codes_ref[p]
     fields = jnp.concatenate(
         [
@@ -66,15 +67,15 @@
 
 def step_kernel(
     side, groups, chunks,
-    states_ref, norm_gain_ref, final_gain_ref, gate_w, up_w, down_w, proj_w,
+    states_ref, norm_gain_ref, final_gain_ref, gate_hbm, up_hbm, down_hbm, proj_w,
     blk_ref, lens_ref, lane_ref, codes_ref, bucket_ref, tables_ref, which_ref, tab_hbm,
     loss_ref, gate_out, up_out, down_out, proj_out,
-    tab, docs, rows_ref, slope_ref, gelu_ref, hidden_ref, part, part_own, part_tmp, part_in, out_ref,
+    tab, gate_w, up_w, down_w, docs, rows_ref, slope_ref, gelu_ref, hidden_ref, part, part_own, part_tmp, part_in, out_ref,
     final_t, proj_ref, asks, asks_smem, queries, pull_out, score_out, pull_ref, score_ref,
     weights, douts, rows_t, douts_t, dgate, dup, first, twin, held,
     tmp_one, in_one, mids, tmp_two, in_two,
     proj_term, twin_proj, held_proj, land_proj, rows_sum, land_grp,
-    tab_sem, asks_sem, rows_send, rows_recv, dout_send, dout_recv,
+    tab_sem, weight_sem, asks_sem, rows_send, rows_recv, dout_send, dout_recv,
     grp_send, grp_recv, docs_send, docs_recv, ring_send, ring_recv,
     asks_send, asks_recv, pull_send, pull_recv, score_send, score_recv,
     twin_send, twin_recv, chip_send, chip_recv,
@@ -95,7 +96,11 @@
         )
         for i in range(pieces)
     ]
-    for copy in table_copies:
+    weight_copies = [
+        pltpu.make_async_copy(src, dst, weight_sem.at[n])
+        for n, (src, dst) in enumerate(((gate_hbm, gate_w), (up_hbm, up_w), (down_hbm, down_w)))
+    ]
+    for copy in table_copies + weight_copies:
         copy.start()
 
     def to(step):
@@ -283,6 +288,8 @@
     def feed_forward():
         rows_copy(2, True).wait_recv()
         rows_copy(3, True).wait_recv()
+        for copy in weight_copies:
+            copy.wait()
 
         def block(r, carry):
             normed = rows_ref[r]
@@ -325,11 +332,16 @@
 
     def chunk_of(c, carry):
         def passage(i, carry):
-            p = c * span + i
-            docs[grp, p] = rebuild_passage(p, blk_ref, lane_ref, codes_ref, bucket_ref, tab)
+            p = c * span + 2 * i
+            both = [
+                rebuild_passage(p + n, blk_ref, lane_ref, codes_ref, bucket_ref, tab)
+                for n in range(2)
+            ]
+            for n in range(2):
+                docs[grp, p + n] = both[n]
             return carry
 
-        lax.fori_loop(0, span, passage, 0)
+        lax.fori_loop(0, span // 2, passage, 0)
         docs_own(c)
         pl.when(c > 0)(lambda: docs_forward(c - 1))
         pl.when(c == 0)(feed_forward)
@@ -366,30 +378,40 @@
 
     lax.fori_loop(0, chunks, docs_in, 0)
 
-    def serve(step, carry):
-        d = source(step)
-        rows = []
+    def answer(d):
+        found = []
         for k in range(caps):
             p = asks_smem[d, 0, k]
             raw = jnp.concatenate([docs[g, p] for g in range(groups)], axis=0)
-            pull, score = pair(raw, queries[d // 2, d % 2, asks_smem[d, 0, caps + k]], lens_ref[p])
-            pull_out[d, k] = pull
-            rows.append(jnp.broadcast_to(score, (1, dim)))
-        score_out[d] = jnp.concatenate(rows + [jnp.zeros((8 - caps, dim), jnp.float32)], axis=0)
-
-        @pl.when(step > 0)
-        def _():
-            pull_copy(step, me).start()
-            score_copy(step, me).start()
-
-        @pl.when(step == 0)
+            unit = queries[d // 2, d % 2, asks_smem[d, 0, caps + k]]
+            found.append(pair(raw, unit, lens_ref[p]))
+        return found
+
+    def serve(i, carry):
+        found = [answer(source(2 * i + n)) for n in range(2)]
+        for n in range(2):
+            d = source(2 * i + n)
+            for k in range(caps):
+                pull_out[d, k] = found[n][k][0]
+            rows = [jnp.broadcast_to(found[n][k][1], (1, dim)) for k in range(caps)]
+            score_out[d] = jnp.concatenate(
+                rows + [jnp.zeros((8 - caps, dim), jnp.float32)], axis=0
+            )
+        for n in range(2):
+
+            @pl.when(2 * i + n > 0)
+            def _():
+                pull_copy(2 * i + n, me).start()
+                score_copy(2 * i + n, me).start()
+
+        @pl.when(i == 0)
         def _():
             pull_ref[me] = pull_out[me]
             score_ref[me] = score_out[me]
 
         return carry
 
-    lax.fori_loop(0, shards, serve, 0)
+    lax.fori_loop(0, shards // 2, serve, 0)
 
     for r in range(groups):
         turned = rows_ref[r].T.reshape(side * side, 2, rows_t.shape[2], tok_rows)
@@ -669,6 +691,7 @@
     spread = jnp.broadcast_to(bucket[:, :, None], (4, dims, toks))
     vmem = pl.BlockSpec(memory_space=pltpu.VMEM)
     smem = pl.BlockSpec(memory_space=pltpu.SMEM)
+    hbm = pl.BlockSpec(memory_space=pl.ANY)
     bf16, f32 = jnp.bfloat16, jnp.float32
     dma = pltpu.SemaphoreType.DMA
     wide = (side, side, block, -(-3 * part // 256) * 256)
@@ -678,10 +701,13 @@
         out_shape=(jax.ShapeDtypeStruct((8, 128), f32),)
         + (jax.ShapeDtypeStruct((block, part), f32),) * 3
         + (jax.ShapeDtypeStruct((block // groups, dim), f32),),
-        in_specs=[vmem] * 7 + [smem] * 2 + [vmem] * 5 + [pl.BlockSpec(memory_space=pl.ANY)],
+        in_specs=[vmem] * 3 + [hbm] * 3 + [vmem] + [smem] * 2 + [vmem] * 5 + [hbm],
         out_specs=(vmem,) * 5,
         scratch_shapes=[
             pltpu.VMEM((dims, count), bf16),
+            pltpu.VMEM((part, width), bf16),
+            pltpu.VMEM((part, width), bf16),
+            pltpu.VMEM((part, width), bf16),
             pltpu.VMEM((groups, passages, dims, toks), bf16),
             pltpu.VMEM((groups, tok_rows, width), bf16),
             pltpu.VMEM((groups, tok_rows, part), bf16),
@@ -722,6 +748,7 @@
             pltpu.VMEM((groups, block // groups, dim), f32),
             pltpu.VMEM((groups - 1, block // groups, dim), f32),
             dma((8,)),
+            dma((3,)),
             dma,
         ]
         + [dma((groups,))] * 6

time: 170 us -> 166 us (0.976)
  Pallas kernels: 154 us -> 150 us
    pallas_call x1, Pallas kernels: 154 us -> 150 us  [step_call(): pl.pallas_call(functools.partial(step_kernel, side, groups, chunks), out_...]
where the time goes in v5:
time: 166 us; the launch traced here: 165 us
  Pallas kernels  150 us (90%)
  local copies, waits for them, and re-layouts  11.5 us (7%)
  other arithmetic  2.77 us (2%)
    pallas_call x1, Pallas kernels, step_call(): pl.pallas_call(functools.partial(step_kernel, side, groups, chunks), out_...  150 us
    unnamed x4, local copies, waits for them, and re-layouts  5.88 us

profile of v5, /device:TPU:0, one launch (start us, length us, event | category | flops | bytes accessed | tf_op | source)
XLA Modules:
  0.0 165.5 jit_solution(5593224782311727889)
XLA Ops:
  0.6 1.3 dynamic_slice.3.lens_ref
  1.9 0.8 reshape.171
  2.7 0.1 pad.7.clone
  2.8 0.1 convolution_convert_fusion
  2.9 0.1 fusion.1
  3.1 0.2 select_reduce_fusion.1
  3.3 0.1 copy.23
  3.4 0.1 copy.22
  3.5 0.1 copy.18
  3.6 0.7 add_add_fusion
  4.3 0.2 convert_add_fusion
  4.5 0.6 pad_bitcast_fusion.which_ref
  5.1 1.4 broadcast_in_dim.33.bucket_ref
  6.5 1.5 broadcast_and_fusion
  8.0 150.4 %shard_map.164 = (f32[8,128]{1,0:T(8,128)}, f32[32,656]{1,0:T(8,128)}, f32[32,656]{1,0:T(8,128)}, f32[32,656]{1,0:T(8,128)}, f32[8,128]{1,0:T(8,128)}) custom-call(bf16[128,1024]{1,0:T(8,128)(2,1)} %bitcast.14, f32[1,1024]{1,0:T(1,128)} %bitcast.16, f32[1,1024]{1,0:T(1,128)} %bitcast.17, bf16[656,1024]{1,0:T(8,128)(2,1)} %bitcast.11, ...), custom_call_target="tpu_custom_call" | custom-call | bytes 300000000 | tf_op jit(solution)/shard_map/pallas_call | solution.py:699
  158.4 1.2 slice_bitcast_fusion
  159.6 1.5 copy.28
  161.1 1.5 copy.29
  162.6 1.5 copy.30
  164.2 1.3 copy.31
  (5 shorter events, 0.1 us)

commit v6 on v5

--- a/solution.py
+++ b/solution.py
@@ -21,7 +21,7 @@
     dims, toks = tab.shape[0], lane_ref.shape[1]
     lane = lax.broadcasted_iota(jnp.int32, (dims, toks), 1)
     shift = 2 * lax.broadcasted_iota(jnp.int32, (8, toks), 0)
-    spot = jnp.broadcast_to(lane_ref[pl.ds(p, 1), :], (dims, toks))
+    spot = jnp.broadcast_to(jnp.bitwise_and(lane_ref[pl.ds(p, 1), :], 127), (dims, toks))
     base = jnp.zeros((dims, toks), jnp.float32)
     for j in range(toks):
         block = tab[:, pl.ds(blk_ref[p, j] * 128, 128)].astype(jnp.float32)
@@ -68,9 +68,9 @@
 def step_kernel(
     side, groups, chunks,
     states_ref, norm_gain_ref, final_gain_ref, gate_hbm, up_hbm, down_hbm, proj_w,
-    blk_ref, lens_ref, lane_ref, codes_ref, bucket_ref, tables_ref, which_ref, tab_hbm,
+    blk_ref, lens_ref, lane_ref, codes_ref, levels_ref, tables_ref, which_ref, tab_hbm,
     loss_ref, gate_out, up_out, down_out, proj_out,
-    tab, gate_w, up_w, down_w, docs, rows_ref, slope_ref, gelu_ref, hidden_ref, part, part_own, part_tmp, part_in, out_ref,
+    tab, bucket_ref, gate_w, up_w, down_w, docs, rows_ref, slope_ref, gelu_ref, hidden_ref, part, part_own, part_tmp, part_in, out_ref,
     final_t, proj_ref, asks, asks_smem, queries, pull_out, score_out, pull_ref, score_ref,
     weights, douts, rows_t, douts_t, dgate, dup, first, twin, held,
     tmp_one, in_one, mids, tmp_two, in_two,
@@ -113,6 +113,9 @@
             ((z + side - dz) % side) * side + (x + side - dx) % side
         ) * 2 + (core + 2 - dc) % 2
 
+    for level in range(4):
+        row = levels_ref[level : level + 1, :]
+        bucket_ref[level] = jnp.broadcast_to(row, (toks, row.shape[1])).T
     barrier = pltpu.get_barrier_semaphore()
 
     def greet(step, carry):
@@ -688,7 +691,6 @@
     chunks = 8
     block = width // shards
     tokens = groups * tok_rows
-    spread = jnp.broadcast_to(bucket[:, :, None], (4, dims, toks))
     vmem = pl.BlockSpec(memory_space=pltpu.VMEM)
     smem = pl.BlockSpec(memory_space=pltpu.SMEM)
     hbm = pl.BlockSpec(memory_space=pl.ANY)
@@ -705,6 +707,7 @@
         out_specs=(vmem,) * 5,
         scratch_shapes=[
             pltpu.VMEM((dims, count), bf16),
+            pltpu.VMEM((4, dims, toks), f32),
             pltpu.VMEM((part, width), bf16),
             pltpu.VMEM((part, width), bf16),
             pltpu.VMEM((part, width), bf16),
@@ -763,7 +766,7 @@
         cost_estimate=pl.CostEstimate(flops=0, bytes_accessed=300_000_000, transcendentals=0),
     )(
         states, norm_gain, final_gain, w_gate, w_up, w_down_t, w_proj, cent_ids >> 7, lens,
-        cent_ids & 127, codes, spread, tables, which, table,
+        cent_ids, codes, bucket, tables, which, table,
     )
 
 

time: 166 us -> 164 us (0.988)
  no operation moved by 1% of the time
where the time goes in v6:
time: 164 us
  Pallas kernels  150 us (91%)
  local copies, waits for them, and re-layouts  10.1 us (6%)
  other arithmetic  2.75 us (2%)
    pallas_call x1, Pallas kernels, step_call(): pl.pallas_call(functools.partial(step_kernel, side, groups, chunks), out_...  150 us
    unnamed x4, local copies, waits for them, and re-layouts  5.89 us

profile of v6, /device:TPU:0, one launch (start us, length us, event | category | flops | bytes accessed | tf_op | source)
XLA Modules:
  0.0 164.1 jit_solution(8466888066403285824)
XLA Ops:
  0.6 1.3 dynamic_slice.3.lens_ref
  1.9 0.8 reshape.170
  2.7 0.1 pad.7.clone
  2.8 0.1 convolution_convert_fusion
  2.9 0.1 fusion.1
  3.1 0.2 select_reduce_fusion.1
  3.3 0.1 copy.23
  3.4 0.1 copy.22
  3.5 0.1 copy.18
  3.6 0.7 add_add_fusion
  4.3 0.2 convert_add_fusion
  4.5 0.6 pad_bitcast_fusion.which_ref
  5.1 1.5 broadcast_shift-right-arithmetic_fusion.blk_ref
  6.6 150.4 %shard_map.164 = (f32[8,128]{1,0:T(8,128)}, f32[32,656]{1,0:T(8,128)}, f32[32,656]{1,0:T(8,128)}, f32[32,656]{1,0:T(8,128)}, f32[8,128]{1,0:T(8,128)}) custom-call(bf16[128,1024]{1,0:T(8,128)(2,1)} %bitcast.14, f32[1,1024]{1,0:T(1,128)} %bitcast.16, f32[1,1024]{1,0:T(1,128)} %bitcast.17, bf16[656,1024]{1,0:T(8,128)(2,1)} %bitcast.11, ...), custom_call_target="tpu_custom_call" | custom-call | bytes 300000000 | tf_op jit(solution)/shard_map/pallas_call | solution.py:701
  157.0 1.2 slice_bitcast_fusion
  158.2 1.5 copy.28
  159.7 1.5 copy.29
  161.3 1.5 copy.30
  162.8 1.3 copy.31
  (5 shorter events, 0.1 us)
